TPU v7x, 32 devices: a whole 2x2x4 slice. The times are simulated.
32 devices in a mesh: tok: 4 (over x, core), hid: 8 (over z, y).
Axes of the slice: x: 2, y: 2, z: 4, core: 2. Of those that a mesh axis runs over, the one named last changes fastest.
Arguments:
- layer_input: bfloat16 [3072, 5120], P(('tok', 'hid')), may hold values from -6 to 6
- output_grad: bfloat16 [3072, 5120], P(('tok', 'hid')), may hold values from -6 to 6
- gate_weight: bfloat16 [5120, 8192], P(None, 'hid'), may hold values from -0.078125 to 0.078125
- up_weight: bfloat16 [5120, 8192], P(None, 'hid'), may hold values from -0.078125 to 0.078125
- down_weight: bfloat16 [8192, 5120], P('hid'), may hold values from -0.0625 to 0.0625
- block_lists: int32 [24, 32], P('tok'), may hold values from 0 to 63, as said below
- block_count: int32 [24], P('tok'), may hold values from 8 to 32, as said below
Outputs:
- input_grad: bfloat16 [3072, 5120], P(('tok', 'hid'))
- gate_grad: bfloat16 [5120, 8192], P('tok', 'hid')
- up_grad: bfloat16 [5120, 8192], P('tok', 'hid')
- down_grad: bfloat16 [8192, 5120], P('hid', 'tok')
Inputs may be any that keep to these rules, and one draw needn't show every extreme that they name: Each row of block_lists holds 32 different block numbers; entries past the tile's count are valid block numbers too and are not active. `block_count`: some tile uses all 32 slots and some tile uses 8.
All inputs are finite; a program needn't handle non-finite values.
Results may differ from a plain program's by a relative error of at most 0.015.
Values may be sent and summed in bfloat16 or wider, within the bound.
A program may use at most 192 MiB of HBM per device.

v0:
```python
import math

import jax
import jax.numpy as jnp
from jax import lax
from jax.sharding import PartitionSpec as P

BLOCK = 128
TILE = 128


def tile_activity(block_lists, block_count, local_blocks):
    in_list = jnp.arange(block_lists.shape[1])[None, :] < block_count[:, None]
    hits = (block_lists[:, :, None] == local_blocks[None, None, :]) & in_list[:, :, None]
    return jnp.any(hits, axis=1)


def unit_grads(gate_pre, up_pre, grad_hidden, unit_mask):
    sigmoid_g = jax.nn.sigmoid(gate_pre)
    silu_g = gate_pre * sigmoid_g
    hidden = (unit_mask * silu_g * up_pre).astype(jnp.bfloat16)
    grad_gate = (
        unit_mask * grad_hidden * up_pre * sigmoid_g * (1.0 + gate_pre * (1.0 - sigmoid_g))
    ).astype(jnp.bfloat16)
    grad_up = (unit_mask * grad_hidden * silu_g).astype(jnp.bfloat16)
    return (hidden, grad_gate, grad_up)


def body(layer_input, output_grad, gate_weight, up_weight, down_weight, block_lists, block_count):
    contract_last = (((1,), (1,)), ((), ()))
    contract_first = (((0,), (0,)), ((), ()))
    width = gate_weight.shape[1]
    blocks_here = width // BLOCK
    local_blocks = lax.axis_index("hid") * blocks_here + jnp.arange(blocks_here, dtype=jnp.int32)
    active = tile_activity(block_lists, block_count, local_blocks)
    inputs_full = lax.all_gather(layer_input, "hid", axis=0, tiled=True)
    grads_full = lax.all_gather(output_grad, "hid", axis=0, tiled=True)
    tok_rows = inputs_full.shape[0]
    tiles_here = tok_rows // TILE
    unit_mask = jnp.broadcast_to(
        active.astype(jnp.float32)[:, None, :, None], (tiles_here, TILE, blocks_here, BLOCK)
    ).reshape(tok_rows, width)
    gate_pre = jnp.dot(inputs_full, gate_weight, preferred_element_type=jnp.float32)
    up_pre = jnp.dot(inputs_full, up_weight, preferred_element_type=jnp.float32)
    grad_hidden = lax.dot_general(
        grads_full, down_weight, contract_last, preferred_element_type=jnp.float32
    )
    hidden, grad_gate, grad_up = unit_grads(gate_pre, up_pre, grad_hidden, unit_mask)
    total = lax.dot_general(
        grad_gate, gate_weight, contract_last, preferred_element_type=jnp.float32
    )
    input_grad = lax.psum_scatter(
        (
            total
            + lax.dot_general(grad_up, up_weight, contract_last, preferred_element_type=jnp.float32)
        ).astype(jnp.bfloat16),
        "hid",
        scatter_dimension=0,
        tiled=True,
    )
    scale = 1.0 / math.sqrt(tok_rows * lax.axis_size("tok"))
    inputs_cols, grads_cols = (
        lax.all_to_all(inputs_full, "tok", split_axis=1, concat_axis=0, tiled=True),
        lax.all_to_all(grads_full, "tok", split_axis=1, concat_axis=0, tiled=True),
    )
    sum_gate = lax.dot_general(
        inputs_cols,
        lax.all_gather(grad_gate, "tok", axis=0, tiled=True),
        contract_first,
        preferred_element_type=jnp.float32,
    )
    sum_up = lax.dot_general(
        inputs_cols,
        lax.all_gather(grad_up, "tok", axis=0, tiled=True),
        contract_first,
        preferred_element_type=jnp.float32,
    )
    sum_down = lax.dot_general(
        grads_cols,
        lax.all_gather(hidden, "tok", axis=0, tiled=True),
        contract_first,
        preferred_element_type=jnp.float32,
    )
    sum_gate, sum_up, sum_down = (sum_gate, sum_up, sum_down)
    gate_grad = (sum_gate * scale).astype(jnp.bfloat16)
    up_grad = (sum_up * scale).astype(jnp.bfloat16)
    down_grad = (sum_down * scale).T.astype(jnp.bfloat16)
    return (input_grad, gate_grad, up_grad, down_grad)


def solution(mesh):
    in_specs = (
        P(("tok", "hid"), None),
        P(("tok", "hid"), None),
        P(None, "hid"),
        P(None, "hid"),
        P("hid", None),
        P("tok", None),
        P("tok"),
    )
    out_specs = (P(("tok", "hid"), None), P("tok", "hid"), P("tok", "hid"), P("hid", "tok"))
    return jax.shard_map(body, mesh=mesh, in_specs=in_specs, out_specs=out_specs, check_vma=False)
```

profile of v0, /device:TPU:0, one launch (start us, length us, event | category | flops | bytes accessed | tf_op | source)
XLA Modules:
  0.0 665.6 jit_solution(11190626084224969052)
XLA Ops:
  7.2 0.7 all-gather.8.cloned.1.call-update
  7.9 0.0 all-gather.6.cloned.1.call-start
  7.9 0.7 all-gather.6.cloned.1.call-update
  8.6 0.0 all-gather.10.cloned.1.call-start
  8.7 0.7 iota_compare_fusion
  9.4 0.9 and_reduce_fusion
  10.4 120.9 %all-gather.8.cloned.1.call-done = bf16[768,5120]{1,0:T(8,128)(2,1)} async-done(((bf16[96,5120]{1,0:T(8,128)(2,1)}), bf16[768,5120]{1,0:T(8,128)(2,1)}) %all-gather.8.cloned.1.call-update) | async-done | bytes 7864336 | tf_op jit(solution)/shard_map/all_gather | solution.py:36
  131.3 14.4 %fusion.5 = f32[768,1024]{1,0:T(8,128)} fusion(bf16[768,5120]{1,0:T(8,128)(2,1)} %all-gather.8.cloned.1.call-done, bf16[5120,1024]{1,0:T(8,128)(2,1)} %param.9), kind=kOutput, calls=%fused_computation.17 | convolution fusion | flops 8053063680 | bytes 21495808 | tf_op jit(solution)/shard_map/dot_general | solution.py:43
  145.7 104.4 %all-gather.6.cloned.1.call-done = bf16[768,5120]{1,0:T(8,128)(2,1)} async-done(((bf16[96,5120]{1,0:T(8,128)(2,1)}), bf16[768,5120]{1,0:T(8,128)(2,1)}) %all-gather.6.cloned.1.call-update) | async-done | bytes 7864336 | tf_op jit(solution)/shard_map/all_gather | solution.py:37
  250.1 2.0 broadcast_in_dim.2
  252.1 16.2 %bitcast_multiply_fusion.1 = f32[768,1024]{1,0:T(8,128)} fusion(f32[96,8,8,128]{3,2,1,0:T(8,128)} %bitcast.42, bf16[768,5120]{1,0:T(8,128)(2,1)} %all-gather.6.cloned.1.call-done, bf16[1024,5120]{1,0:T(8,128)(2,1)} %param.11), kind=kOutput, calls=%fused_computation.7 | convolution fusion | flops 8053850112 | bytes 24641536 | tf_op jit(solution)/shard_map/dot_general | solution.py:45
  268.4 16.9 %fusion.3 = (bf16[768,1024]{1,0:T(8,128)(2,1)}, bf16[768,1024]{1,0:T(8,128)(2,1)}, bf16[768,1024]{1,0:T(8,128)(2,1)}) fusion(f32[96,8,8,128]{3,2,1,0:T(8,128)} %bitcast.43, f32[768,1024]{1,0:T(8,128)} %fusion.5, f32[768,1024]{1,0:T(8,128)} %bitcast_multiply_fusion.1, bf16[768,5120]{1,0:T(8,128)(2,1)S(1)} %bitcast.38, bf16[5120,1024]{1,0:T(8,128)(2,1)} %param.10), kind=kOutput, calls=%fused_computation.9 | convolution fusion | flops 8065646592 | bytes 32505856 | tf_op jit(solution)/shard_map/dot_general | solution.py:44
  285.3 0.0 all-gather.12.cloned.1.call-start
  285.4 0.5 all-gather.12.cloned.1.call-update
  285.9 0.5 all-gather.14.cloned.1.call-update
  286.5 10.8 %copy.29 = bf16[768,5120]{0,1:T(8,128)(2,1)} copy(bf16[768,5120]{1,0:T(8,128)(2,1)} %all-gather.6.cloned.1.call-done) | data formatting | bytes 15728640 | tf_op jit(solution)/shard_map/all_gather | solution.py:37
  297.3 5.7 all-to-all-start.1
  303.1 0.2 reduce-scatter.2.cloned.1.call-start
  303.3 15.3 %fusion.6 = f32[768,5120]{1,0:T(8,128)} fusion(bf16[768,1024]{1,0:T(8,128)(2,1)S(1)} %copy-done.1, bf16[5120,1024]{1,0:T(8,128)(2,1)} %param.9), kind=kOutput, calls=%fused_computation.18 | convolution fusion | flops 8053063680 | bytes 27787264 | tf_op jit(solution)/shard_map/dot_general | solution.py:49
  318.6 16.4 %add_convert_fusion = bf16[768,5120]{1,0:T(8,128)(2,1)} fusion(f32[768,5120]{1,0:T(8,128)} %fusion.6, bf16[768,1024]{1,0:T(8,128)(2,1)S(1)} %copy-done, bf16[5120,1024]{1,0:T(8,128)(2,1)} %param.10), kind=kOutput, calls=%fused_computation | convolution fusion | flops 8060928000 | bytes 35651584 | tf_op jit(solution)/shard_map/dot_general | solution.py:55
  335.0 10.6 %copy.27 = bf16[768,5120]{0,1:T(8,128)(2,1)} copy(bf16[768,5120]{1,0:T(8,128)(2,1)} %all-gather.8.cloned.1.call-done) | data formatting | bytes 15728640 | tf_op jit(solution)/shard_map/all_gather | solution.py:36
  345.6 100.8 %all-to-all-done.1 = bf16[768,4,1280]{0,2,1:T(8,128)(2,1)} async-done(((bf16[768,4,1280]{0,2,1:T(8,128)(2,1)}), bf16[768,4,1280]{0,2,1:T(8,128)(2,1)}, u32[]{:S(2)}, u32[]{:S(2)}) %all-to-all-start.1) | async-done | bytes 7864352 | tf_op jit(solution)/shard_map/all_to_all | solution.py:64
  446.4 6.1 all-to-all-start
  452.5 10.3 %copy.30 = bf16[4,768,1280]{2,1,0:T(8,128)(2,1)} copy(bf16[4,768,1280]{1,2,0:T(8,128)(2,1)} %bitcast.6) | data formatting | bytes 15728640 | tf_op jit(solution)/shard_map/all_to_all | solution.py:64
  462.9 105.5 %all-to-all-done = bf16[768,4,1280]{0,2,1:T(8,128)(2,1)} async-done(((bf16[768,4,1280]{0,2,1:T(8,128)(2,1)}), bf16[768,4,1280]{0,2,1:T(8,128)(2,1)}, u32[]{:S(2)}, u32[]{:S(2)}) %all-to-all-start) | async-done | bytes 7864352 | tf_op jit(solution)/shard_map/all_to_all | solution.py:63
  568.4 10.8 %copy.28 = bf16[4,768,1280]{2,1,0:T(8,128)(2,1)} copy(bf16[4,768,1280]{1,2,0:T(8,128)(2,1)} %bitcast.1) | data formatting | bytes 15728640 | tf_op jit(solution)/shard_map/all_to_all | solution.py:63
  579.1 12.9 %fusion = bf16[1280,1024]{0,1:T(8,128)(2,1)S(1)} fusion(bf16[3072,1024]{1,0:T(8,128)(2,1)} %all-gather.10.cloned.1.call-done, bf16[3072,1280]{1,0:T(8,128)(2,1)} %bitcast.40), kind=kOutput, calls=%fused_computation.4 | convolution fusion | flops 8055685120 | bytes 16777216 | tf_op jit(solution)/shard_map/dot_general | solution.py:66
  592.1 2.6 copy.31
  594.7 12.8 %fusion.1 = bf16[1280,1024]{0,1:T(8,128)(2,1)S(1)} fusion(bf16[3072,1024]{1,0:T(8,128)(2,1)} %all-gather.12.cloned.1.call-done, bf16[3072,1280]{1,0:T(8,128)(2,1)} %bitcast.41), kind=kOutput, calls=%fused_computation.5 | convolution fusion | flops 8055685120 | bytes 16777216 | tf_op jit(solution)/shard_map/dot_general | solution.py:72
  607.5 2.6 copy.32
  610.1 13.9 %multiply_convert_fusion = bf16[1024,1280]{1,0:T(8,128)(2,1)} fusion(bf16[3072,1024]{1,0:T(8,128)(2,1)} %all-gather.14.cloned.1.call-done, bf16[3072,1280]{1,0:T(8,128)(2,1)} %bitcast.39), kind=kOutput, calls=%fused_computation.1 | convolution fusion | flops 8055685120 | bytes 16777216 | tf_op jit(solution)/shard_map/dot_general | solution.py:78
  624.0 34.7 %reduce-scatter.2.cloned.1.call-done = bf16[96,5120]{1,0:T(8,128)(2,1)} async-done(((bf16[768,5120]{1,0:T(8,128)(2,1)}), bf16[96,5120]{1,0:T(8,128)(2,1)}) %reduce-scatter.2.cloned.1.call-update) | async-done | bytes 983056 | tf_op jit(solution)/shard_map/reduce_scatter | solution.py:52
  (18 shorter events, 0.1 us)
Async XLA Ops:
  7.2 124.2 %all-gather.8.cloned.1.call-start = ((), (), s32[]{:S(2)}) async-start(), calls=%async_computation.4 | async-start | bytes 8847360 | tf_op jit(solution)/shard_map/all_gather | solution.py:36
  7.9 242.2 %all-gather.6.cloned.1.call-start = ((), (), s32[]{:S(2)}) async-start(), calls=%async_computation.3 | async-start | bytes 8847360 | tf_op jit(solution)/shard_map/all_gather | solution.py:37
  8.6 570.5 %all-gather.10.cloned.1.call-start = ((), (), s32[]{:S(2)}) async-start(), calls=%async_computation.6 | async-start | bytes 7864320 | tf_op jit(solution)/shard_map/all_gather | solution.py:68
  250.1 18.3 %slice-start = ((s8[7864320]{0:T(1024)(128)(4,1)}), s8[4194304]{0:T(1024)(128)(4,1)S(1)}, s32[]{:S(2)}) async-start(s8[7864320]{0:T(1024)(128)(4,1)} %bitcast.37), calls=%async_computation.9 | async-start | bytes 8388608
  252.1 16.2 %slice-start.1 = ((s8[7864320]{0:T(1024)(128)(4,1)}), s8[3670016]{0:T(1024)(128)(4,1)S(1)}, s32[]{:S(2)}) async-start(s8[7864320]{0:T(1024)(128)(4,1)} %bitcast.37), calls=%async_computation.10 | async-start | bytes 7340032
  285.3 309.4 %all-gather.12.cloned.1.call-start = ((), (), s32[]{:S(2)}) async-start(), calls=%async_computation.7 | async-start | bytes 7864320 | tf_op jit(solution)/shard_map/all_gather | solution.py:74
  285.9 324.2 %all-gather.14.cloned.1.call-start = ((), (), s32[]{:S(2)}) async-start(), calls=%async_computation.8 | async-start | bytes 7864320 | tf_op jit(solution)/shard_map/all_gather | solution.py:80
  297.3 6.0 copy-start.1
  297.3 149.1 %all-to-all-start.1 = ((bf16[768,4,1280]{0,2,1:T(8,128)(2,1)}), bf16[768,4,1280]{0,2,1:T(8,128)(2,1)}, u32[]{:S(2)}, u32[]{:S(2)}) async-start(bf16[768,4,1280]{0,2,1:T(8,128)(2,1)} %bitcast.35), calls=%async_computation.2 | async-start | bytes 15728640 | tf_op jit(solution)/shard_map/all_to_all | solution.py:64
  303.0 15.6 %copy-start = (bf16[768,1024]{1,0:T(8,128)(2,1)S(1)}, bf16[768,1024]{1,0:T(8,128)(2,1)}, u32[]{:S(2)}) copy-start(bf16[768,1024]{1,0:T(8,128)(2,1)} %get-tuple-element.26) | copy-start | bytes 4718596
  303.1 355.7 %reduce-scatter.2.cloned.1.call-start = ((), (), s32[]{:S(2)}) async-start(), calls=%async_computation.5 | async-start | bytes 8847360 | tf_op jit(solution)/shard_map/reduce_scatter | solution.py:52
  446.4 121.9 %all-to-all-start = ((bf16[768,4,1280]{0,2,1:T(8,128)(2,1)}), bf16[768,4,1280]{0,2,1:T(8,128)(2,1)}, u32[]{:S(2)}, u32[]{:S(2)}) async-start(bf16[768,4,1280]{0,2,1:T(8,128)(2,1)} %bitcast.36), calls=%async_computation.1 | async-start | bytes 15728640 | tf_op jit(solution)/shard_map/all_to_all | solution.py:63
Sparse Core Ops, SparseCore 0:
  10.2 121.0 all-gather.7
  133.5 116.5 all-gather.5
  285.4 66.7 all-gather.9
  353.6 83.5 all-gather.11
  439.3 74.7 all-gather.13
  518.1 140.5 reduce-scatter.1
where the time goes:
time: 667 us; the launch traced here: 666 us
  waiting for transfers between devices  469 us (70%)
  matrix products  119 us (18%)
  local copies, waits for them, and re-layouts  49.8 us (7%)
  between operations  14.2 us (2%)
  starting transfers between devices  12.2 us (2%)
    all_gather x1, waiting for transfers between devices, body(): inputs_full = lax.all_gather(layer_input, 'hid', axis=0, tiled=True)  121 us
    all_to_all x1, waiting for transfers between devices, body(): lax.all_to_all(inputs_full, 'tok', split_axis=1, concat_axis=0, tiled=True)  106 us
    all_gather x1, waiting for transfers between devices, body(): grads_full = lax.all_gather(output_grad, 'hid', axis=0, tiled=True)  104 us
    all_to_all x1, waiting for transfers between devices, body(): lax.all_to_all(grads_full, 'tok', split_axis=1, concat_axis=0, tiled=True)  101 us
    reduce_scatter x1, waiting for transfers between devices, body(): lax.psum_scatter((total + lax.dot_general(grad_up, up_weight, contract_la...  34.7 us
    dot_general x1, matrix products, body(): up_pre = jnp.dot(inputs_full, up_weight, preferred_element_type=jnp.float32)  16.9 us
    dot_general x1, matrix products, body(): lax.dot_general(grad_up, up_weight, contract_last, preferred_element_type...  16.4 us
    dot_general x1, matrix products, body(): lax.dot_general(grads_full, down_weight, contract_last, preferred_element...  16.2 us
  transfers between devices with their start and end apart: 8, of which 5 were waited for; matrix products, arithmetic and copies ran while one was open for 20% of the time, Pallas kernels for 0%

commit v1 on v0

v1 whole, which is shorter than its diff:
```python
import functools
import math

import jax
import jax.numpy as jnp
from jax import lax
from jax.experimental import pallas as pl
from jax.experimental.pallas import tpu as pltpu
from jax.sharding import PartitionSpec as P

BLOCK = 128
TILE = 128
MESH = pl.DeviceIdType.MESH


def partner(t, j, n_tok):
    p = (t + (j // 2) * 2) % n_tok
    if j % 2:
        p = p + 1 - 2 * (p % 2)
    return p


def gather_kernel(n_tok, n_hid, x_ref, g_ref, xf, gf, xc, gc, local_sem, ag_send, ag_recv, col_send, col_recv):
    t = lax.axis_index("tok")
    h = lax.axis_index("hid")
    lines = n_hid // 2
    z, y = h // 2, h % 2
    width = xc.shape[3]
    fulls, cols, mine = (xf, gf), (xc, gc), (x_ref, g_ref)

    barrier = pltpu.get_barrier_semaphore()
    other = z * 2 + 1 - y
    pl.semaphore_signal(barrier, inc=1, device_id=(t, other), device_id_type=MESH)

    @pl.when(z > 0)
    def _():
        pl.semaphore_signal(barrier, inc=1, device_id=(t, h - 2), device_id_type=MESH)

    @pl.when(z < lines - 1)
    def _():
        pl.semaphore_signal(barrier, inc=1, device_id=(t, h + 2), device_id_type=MESH)

    for j in range(1, n_tok):
        pl.semaphore_signal(barrier, inc=1, device_id=(partner(t, j, n_tok), h), device_id_type=MESH)
    pl.semaphore_wait(barrier, n_tok + jnp.where(z > 0, 1, 0) + jnp.where(z < lines - 1, 1, 0))

    def ag(a, src, s, way, dev):
        return pltpu.make_async_remote_copy(
            src_ref=src, dst_ref=fulls[a].at[s], send_sem=ag_send.at[a, way, s], recv_sem=ag_recv.at[a, s],
            device_id=(t, dev), device_id_type=MESH,
        )

    def col(a, src, s, j):
        p = partner(t, j, n_tok)
        return pltpu.make_async_remote_copy(
            src_ref=src.at[:, pl.ds(pl.multiple_of(p * width, 128), width)],
            dst_ref=cols[a].at[j, s],
            send_sem=col_send.at[a, j, s], recv_sem=col_recv.at[a, j, s],
            device_id=(p, h), device_id_type=MESH,
        )

    def own(a, src, s):
        return pltpu.make_async_copy(
            src.at[:, pl.ds(pl.multiple_of(t * width, 128), width)], cols[a].at[0, s], local_sem.at[a, s]
        )

    def full_own(a):
        return pltpu.make_async_copy(mine[a], fulls[a].at[h], local_sem.at[a, n_hid])

    def send_cols(a, src, s):
        for j in range(2, n_tok):
            col(a, src, s, j).start()
        col(a, src, s, 1).start()
        own(a, src, s).start()

    for a in range(2):
        src = mine[a]

        @pl.when(z < lines - 1)
        def _():
            ag(a, src, h, 0, h + 2).start()

        @pl.when(z > 0)
        def _():
            ag(a, src, h, 1, h - 2).start()

        ag(a, src, h, 2, other).start()
    for a in range(2):
        full_own(a).start()
        send_cols(a, mine[a], h)

    for d in range(1, lines):
        for a in range(2):
            @pl.when(z - d >= 0)
            def _():
                s = h - 2 * d
                ag(a, fulls[a].at[s], s, 0, h + 2).wait_recv()

                @pl.when(z < lines - 1)
                def _():
                    ag(a, fulls[a].at[s], s, 0, h + 2).start()

                ag(a, fulls[a].at[s], s, 2, other).start()
                send_cols(a, fulls[a].at[s], s)

            @pl.when(z + d < lines)
            def _():
                s = h + 2 * d
                ag(a, fulls[a].at[s], s, 1, h - 2).wait_recv()

                @pl.when(z > 0)
                def _():
                    ag(a, fulls[a].at[s], s, 1, h - 2).start()

                ag(a, fulls[a].at[s], s, 2, other).start()
                send_cols(a, fulls[a].at[s], s)

        for a in range(2):
            if d == 1:
                ag(a, fulls[a].at[other], other, 2, other).wait_recv()
                send_cols(a, fulls[a].at[other], other)

            @pl.when(z - d >= 0)
            def _():
                s = other - 2 * d
                ag(a, fulls[a].at[s], s, 2, other).wait_recv()
                send_cols(a, fulls[a].at[s], s)

            @pl.when(z + d < lines)
            def _():
                s = other + 2 * d
                ag(a, fulls[a].at[s], s, 2, other).wait_recv()
                send_cols(a, fulls[a].at[s], s)

    for a in range(2):
        full_own(a).wait()
        for zz in range(lines):
            s = zz * 2 + y

            @pl.when(jnp.logical_and(zz <= z, z < lines - 1))
            def _():
                ag(a, fulls[a].at[s], s, 0, h + 2).wait_send()

            @pl.when(jnp.logical_and(zz >= z, z > 0))
            def _():
                ag(a, fulls[a].at[s], s, 1, h - 2).wait_send()

            ag(a, fulls[a].at[s], s, 2, other).wait_send()
        for s in range(n_hid):
            own(a, fulls[a].at[s], s).wait()
            for j in range(1, n_tok):
                col(a, fulls[a].at[s], s, j).wait_send()
                col(a, fulls[a].at[s], s, j).wait_recv()


def gather(layer_input, output_grad, n_tok, n_hid):
    rows, depth = layer_input.shape
    width = depth // n_tok
    full = jax.ShapeDtypeStruct((n_hid, rows, depth), jnp.bfloat16)
    cols = jax.ShapeDtypeStruct((n_tok, n_hid, rows, width), jnp.bfloat16)
    anywhere = pl.BlockSpec(memory_space=pl.ANY)
    return pl.pallas_call(
        functools.partial(gather_kernel, n_tok, n_hid),
        out_shape=(full, full, cols, cols),
        in_specs=[anywhere] * 2,
        out_specs=(anywhere,) * 4,
        scratch_shapes=[
            pltpu.SemaphoreType.DMA((2, n_hid + 1)),
            pltpu.SemaphoreType.DMA((2, 3, n_hid)),
            pltpu.SemaphoreType.DMA((2, n_hid)),
            pltpu.SemaphoreType.DMA((2, n_tok, n_hid)),
            pltpu.SemaphoreType.DMA((2, n_tok, n_hid)),
        ],
        compiler_params=pltpu.CompilerParams(collective_id=0, has_side_effects=True),
        name="gather_rows_and_columns",
    )(layer_input, output_grad)


def unit_grads(gate_pre, up_pre, grad_hidden, unit_mask):
    sigmoid_g = jax.nn.sigmoid(gate_pre)
    silu_g = gate_pre * sigmoid_g
    hidden = (unit_mask * silu_g * up_pre).astype(jnp.bfloat16)
    grad_gate = (
        unit_mask * grad_hidden * up_pre * sigmoid_g * (1.0 + gate_pre * (1.0 - sigmoid_g))
    ).astype(jnp.bfloat16)
    grad_up = (unit_mask * grad_hidden * silu_g).astype(jnp.bfloat16)
    return (hidden, grad_gate, grad_up)


def tile_activity(block_lists, block_count, local_blocks):
    in_list = jnp.arange(block_lists.shape[1])[None, :] < block_count[:, None]
    hits = (block_lists[:, :, None] == local_blocks[None, None, :]) & in_list[:, :, None]
    return jnp.any(hits, axis=1)


def body(layer_input, output_grad, gate_weight, up_weight, down_weight, block_lists, block_count):
    contract_last = (((1,), (1,)), ((), ()))
    contract_first = (((0,), (0,)), ((), ()))
    n_tok, n_hid = lax.axis_size("tok"), lax.axis_size("hid")
    width = gate_weight.shape[1]
    depth = layer_input.shape[1]
    tok_rows = layer_input.shape[0] * n_hid
    blocks_here = width // BLOCK
    local_blocks = lax.axis_index("hid") * blocks_here + jnp.arange(blocks_here, dtype=jnp.int32)
    active = tile_activity(block_lists, block_count, local_blocks)
    inputs_full, grads_full, inputs_cols, grads_cols = gather(layer_input, output_grad, n_tok, n_hid)
    inputs_full = inputs_full.reshape(tok_rows, depth)
    grads_full = grads_full.reshape(tok_rows, depth)
    inputs_cols = inputs_cols.reshape(n_tok * tok_rows, depth // n_tok)
    grads_cols = grads_cols.reshape(n_tok * tok_rows, depth // n_tok)
    tiles_here = tok_rows // TILE
    unit_mask = jnp.broadcast_to(
        active.astype(jnp.float32)[:, None, :, None], (tiles_here, TILE, blocks_here, BLOCK)
    ).reshape(tok_rows, width)
    gate_pre = jnp.dot(inputs_full, gate_weight, preferred_element_type=jnp.float32)
    up_pre = jnp.dot(inputs_full, up_weight, preferred_element_type=jnp.float32)
    grad_hidden = lax.dot_general(
        grads_full, down_weight, contract_last, preferred_element_type=jnp.float32
    )
    acts = unit_grads(gate_pre, up_pre, grad_hidden, unit_mask)
    _, grad_gate, grad_up = acts
    total = lax.dot_general(
        grad_gate, gate_weight, contract_last, preferred_element_type=jnp.float32
    )
    input_grad = lax.psum_scatter(
        (
            total
            + lax.dot_general(grad_up, up_weight, contract_last, preferred_element_type=jnp.float32)
        ).astype(jnp.bfloat16),
        "hid",
        scatter_dimension=0,
        tiled=True,
    )
    over_core = [(i, i + 1 - 2 * (i % 2)) for i in range(n_tok)]
    slots = [[], [], []]
    for k in range(n_tok // 2):
        for i, arr in enumerate(acts):
            if k:
                arr = lax.ppermute(arr, "tok", [(d, (d + 2 * k) % n_tok) for d in range(n_tok)])
            slots[i] += [arr, lax.ppermute(arr, "tok", over_core)]
    scale = 1.0 / math.sqrt(tok_rows * n_tok)
    near = 2 * tok_rows

    def weight_sum(columns, parts):
        first = lax.dot_general(
            columns[:near], jnp.concatenate(parts[:2]), contract_first, preferred_element_type=jnp.float32
        )
        rest = lax.dot_general(
            columns[near:], jnp.concatenate(parts[2:]), contract_first, preferred_element_type=jnp.float32
        )
        return (first + rest) * scale

    gate_grad = weight_sum(inputs_cols, slots[1]).astype(jnp.bfloat16)
    up_grad = weight_sum(inputs_cols, slots[2]).astype(jnp.bfloat16)
    down_grad = weight_sum(grads_cols, slots[0]).T.astype(jnp.bfloat16)
    return (input_grad, gate_grad, up_grad, down_grad)


def solution(mesh):
    in_specs = (
        P(("tok", "hid"), None),
        P(("tok", "hid"), None),
        P(None, "hid"),
        P(None, "hid"),
        P("hid", None),
        P("tok", None),
        P("tok"),
    )
    out_specs = (P(("tok", "hid"), None), P("tok", "hid"), P("tok", "hid"), P("hid", "tok"))
    return jax.shard_map(body, mesh=mesh, in_specs=in_specs, out_specs=out_specs, check_vma=False)
```

time: 667 us -> 449 us (0.67)
  waiting for transfers between devices: 469 us -> 92.9 us
  Pallas kernels: 0 us -> 210 us
  local copies, waits for them, and re-layouts: 49.8 us -> 7.16 us
  starting transfers between devices: 12.2 us -> 4.69 us
    all_gather x5 -> x0, waiting for transfers between devices: 225 us -> none  [the longest x1 121 us: body(): inputs_full = lax.all_gather(layer_input, 'hid', axis=0, tiled=True)]
    pallas_call x0 -> x1, Pallas kernels: none -> 210 us  [gather(): pl.pallas_call(functools.partial(gather_kernel, n_tok, n_hid), out_shape=...]
    all_to_all x2 -> x0, waiting for transfers between devices: 206 us -> none  [the longest x1 106 us: body(): lax.all_to_all(inputs_full, 'tok', split_axis=1, concat_axis=0, tiled=True)]
    ppermute x0 -> x9, waiting for transfers between devices: none -> 92.9 us  [the longest x3 92.9 us: body(): lax.ppermute(arr, 'tok', [(d, (d + 2 * k) % n_tok) for d in range(n_tok)])]
    reduce_scatter x1, waiting for transfers between devices: 34.7 us -> 0.01 us  [body(): lax.psum_scatter((total + lax.dot_general(grad_up, up_weight, contract_la...]
    all_gather x2 -> x0, local copies, waits for them, and re-layouts: 21.5 us -> none  [the longest x1 10.8 us: body(): grads_full = lax.all_gather(output_grad, 'hid', axis=0, tiled=True)]
    all_to_all x2 -> x0, local copies, waits for them, and re-layouts: 21.1 us -> none  [the longest x1 10.8 us: body(): lax.all_to_all(inputs_full, 'tok', split_axis=1, concat_axis=0, tiled=True)]
    all_to_all x2 -> x0, starting transfers between devices: 11.8 us -> none  [the longest x1 6.08 us: body(): lax.all_to_all(inputs_full, 'tok', split_axis=1, concat_axis=0, tiled=True)]
  transfers between devices with their start and end apart: 8 -> 10, of which waited for: 5 -> 3; matrix products, arithmetic and copies ran while one was open for 20% -> 11% of each run, Pallas kernels for 0% -> 0%
where the time goes in v1:
time: 449 us; the launch traced here: 448 us
  Pallas kernels  210 us (47%)
  matrix products  118 us (26%)
  waiting for transfers between devices  92.9 us (21%)
  between operations  14.1 us (3%)
  local copies, waits for them, and re-layouts  7.16 us (2%)
  starting transfers between devices  4.69 us (1%)
    pallas_call x1, Pallas kernels, gather(): pl.pallas_call(functools.partial(gather_kernel, n_tok, n_hid), out_shape=...  210 us
    ppermute x3, waiting for transfers between devices, body(): lax.ppermute(arr, 'tok', [(d, (d + 2 * k) % n_tok) for d in range(n_tok)])  92.9 us
    dot_general x3, matrix products, weight_sum(): lax.dot_general(columns[:near], jnp.concatenate(parts[:2]), contract_firs...  22.1 us
    dot_general x3, matrix products, weight_sum(): lax.dot_general(columns[near:], jnp.concatenate(parts[2:]), contract_firs...  21.4 us
    dot_general x1, matrix products, body(): up_pre = jnp.dot(inputs_full, up_weight, preferred_element_type=jnp.float32)  16.1 us
    dot_general x1, matrix products, body(): lax.dot_general(grad_up, up_weight, contract_last, preferred_element_type...  15.9 us
    dot_general x1, matrix products, body(): lax.dot_general(grad_gate, gate_weight, contract_last, preferred_element_...  15 us
    dot_general x1, matrix products, body(): lax.dot_general(grads_full, down_weight, contract_last, preferred_element...  14.9 us
  transfers between devices with their start and end apart: 10, of which 3 were waited for; matrix products, arithmetic and copies ran while one was open for 11% of the time, Pallas kernels for 0%

profile of v1, /device:TPU:0, one launch (start us, length us, event | category | flops | bytes accessed | tf_op | source)
XLA Modules:
  0.0 448.4 jit_solution(13637884743038082805)
XLA Ops:
  7.2 0.0 reduce-scatter.2.cloned.1.call-start
  7.2 0.7 iota_compare_fusion
  8.0 0.9 and_reduce_fusion
  8.9 210.0 %gather_rows_and_columns.1 = (bf16[8,96,5120]{2,1,0:T(8,128)(2,1)}, bf16[8,96,5120]{2,1,0:T(8,128)(2,1)}, bf16[4,8,96,1280]{3,2,1,0:T(8,128)(2,1)}, bf16[4,8,96,1280]{3,2,1,0:T(8,128)(2,1)}) custom-call(bf16[96,5120]{1,0:T(8,128)(2,1)} %x_ref.1, bf16[96,5120]{1,0:T(8,128)(2,1)} %g_ref.1), custom_call_target="tpu_custom_call" | custom-call | tf_op jit(solution)/shard_map/gather_rows_and_columns/pallas_call | solution.py:162
  218.9 12.2 %fusion.32 = f32[768,1024]{1,0:T(8,128)S(1)} fusion(bf16[768,5120]{1,0:T(8,128)(2,1)} %bitcast.39, bf16[5120,1024]{1,0:T(8,128)(2,1)} %param.9), kind=kOutput, calls=%fused_computation.44 | convolution fusion | flops 8053063680 | bytes 21495808 | tf_op jit(solution)/shard_map/dot_general | solution.py:215
  231.1 0.3 broadcast_in_dim.2
  231.4 14.9 %bitcast_multiply_fusion.1 = f32[768,1024]{1,0:T(8,128)} fusion(f32[96,8,8,128]{3,2,1,0:T(8,128)S(1)} %bitcast.37, bf16[768,5120]{1,0:T(8,128)(2,1)} %bitcast.41, bf16[1024,5120]{1,0:T(8,128)(2,1)} %param.11), kind=kOutput, calls=%fused_computation.5 | convolution fusion | flops 8053850112 | bytes 24641536 | tf_op jit(solution)/shard_map/dot_general | solution.py:217
  246.4 16.1 %fusion.1 = (bf16[768,1024]{1,0:T(8,128)(2,1)S(1)}, bf16[768,1024]{1,0:T(8,128)(2,1)S(1)}, bf16[768,1024]{1,0:T(8,128)(2,1)}) fusion(f32[96,8,8,128]{3,2,1,0:T(8,128)S(1)} %bitcast.38, f32[768,1024]{1,0:T(8,128)S(1)} %fusion.32, f32[768,1024]{1,0:T(8,128)} %bitcast_multiply_fusion.1, bf16[768,5120]{1,0:T(8,128)(2,1)} %bitcast.40, bf16[5120,1024]{1,0:T(8,128)(2,1)} %param.10), kind=kOutput, calls=%fused_computation.7 | convolution fusion | flops 8065646592 | bytes 32505856 | tf_op jit(solution)/shard_map/dot_general | solution.py:216
  262.5 15.0 %fusion.33 = f32[768,5120]{1,0:T(8,128)} fusion(bf16[768,1024]{1,0:T(8,128)(2,1)S(1)} %get-tuple-element.17, bf16[5120,1024]{1,0:T(8,128)(2,1)} %param.9), kind=kOutput, calls=%fused_computation.45 | convolution fusion | flops 8053063680 | bytes 27787264 | tf_op jit(solution)/shard_map/dot_general | solution.py:222
  277.5 15.9 %add_convert_fusion = bf16[768,5120]{1,0:T(8,128)(2,1)} fusion(f32[768,5120]{1,0:T(8,128)} %fusion.33, bf16[768,1024]{1,0:T(8,128)(2,1)} %get-tuple-element.18, bf16[5120,1024]{1,0:T(8,128)(2,1)} %param.10), kind=kOutput, calls=%fused_computation | convolution fusion | flops 8060928000 | bytes 35651584 | tf_op jit(solution)/shard_map/dot_general | solution.py:228
  293.4 0.0 reduce-scatter.2.cloned.1.call-update
  293.4 0.1 collective-permute-start.7
  293.6 2.0 collective-permute-start.3
  295.5 0.3 collective-permute-start.4
  295.9 1.7 collective-permute-start.1
  297.5 0.0 collective-permute-start
  297.5 6.9 %fusion.30 = (bf16[2,8,96,1280]{3,2,1,0:T(8,128)(2,1)S(1)}, bf16[2,8,96,1280]{3,2,1,0:T(8,128)(2,1)S(1)}, bf16[2,8,96,1280]{3,2,1,0:T(8,128)(2,1)S(1)}, bf16[2,8,96,1280]{3,2,1,0:T(8,128)(2,1)S(1)}) fusion(bf16[4,8,96,1280]{3,2,1,0:T(8,128)(2,1)} %get-tuple-element.11, bf16[4,8,96,1280]{3,2,1,0:T(8,128)(2,1)} %get-tuple-element.10), kind=kLoop, calls=%fused_computation.42 | loop fusion | bytes 31457280 | tf_op jit(solution)/shard_map/slice | solution.py:249
  304.4 26.2 %collective-permute-done.7 = bf16[768,1024]{1,0:T(8,128)(2,1)S(1)} collective-permute-done((bf16[768,1024]{1,0:T(8,128)(2,1)S(1)}, bf16[768,1024]{1,0:T(8,128)(2,1)S(1)}, u32[]{:S(2)}, u32[]{:S(2)}) %collective-permute-start.7) | collective-permute-done | bytes 1572896 | tf_op jit(solution)/shard_map/ppermute | solution.py:239
  330.7 0.5 collective-permute-start.8
  331.2 33.3 %collective-permute-done.4 = bf16[768,1024]{1,0:T(8,128)(2,1)} collective-permute-done((bf16[768,1024]{1,0:T(8,128)(2,1)}, bf16[768,1024]{1,0:T(8,128)(2,1)}, u32[]{:S(2)}, u32[]{:S(2)}) %collective-permute-start.4) | collective-permute-done | bytes 1572896 | tf_op jit(solution)/shard_map/ppermute | solution.py:239
  364.5 0.0 collective-permute-start.5
  364.5 33.4 %collective-permute-done.1 = bf16[768,1024]{1,0:T(8,128)(2,1)} collective-permute-done((bf16[768,1024]{1,0:T(8,128)(2,1)S(1)}, bf16[768,1024]{1,0:T(8,128)(2,1)}, u32[]{:S(2)}, u32[]{:S(2)}) %collective-permute-start.1) | collective-permute-done | bytes 1572896 | tf_op jit(solution)/shard_map/ppermute | solution.py:239
  397.9 0.0 collective-permute-start.2
  397.9 8.4 %fusion.9 = f32[1280,1024]{1,0:T(8,128)} fusion(bf16[1536,1280]{1,0:T(8,128)(2,1)S(1)} %bitcast.35, bf16[768,1024]{1,0:T(8,128)(2,1)} %collective-permute-done.3, bf16[768,1024]{1,0:T(8,128)(2,1)} %get-tuple-element.18), kind=kOutput, calls=%fused_computation.15 | convolution fusion | flops 4032823296 | bytes 12320768 | tf_op jit(solution)/shard_map/dot_general | solution.py:245
  406.3 0.0 collective-permute-done
  406.3 7.5 %fusion.2 = f32[1280,1024]{1,0:T(8,128)} fusion(bf16[1536,1280]{1,0:T(8,128)(2,1)S(1)} %bitcast.36, bf16[768,1024]{1,0:T(8,128)(2,1)} %collective-permute-done, bf16[768,1024]{1,0:T(8,128)(2,1)S(1)} %get-tuple-element.17), kind=kOutput, calls=%fused_computation.8 | convolution fusion | flops 4032823296 | bytes 12320768 | tf_op jit(solution)/shard_map/dot_general | solution.py:245
  413.8 0.0 collective-permute-done.6
  413.8 6.2 %fusion.16 = f32[1024,1280]{1,0:T(8,128)} fusion(bf16[1536,1280]{1,0:T(8,128)(2,1)S(1)} %bitcast.34, bf16[768,1024]{1,0:T(8,128)(2,1)S(1)} %collective-permute-done.6, bf16[768,1024]{1,0:T(8,128)(2,1)S(1)} %get-tuple-element.16), kind=kOutput, calls=%fused_computation.22 | convolution fusion | flops 4032823296 | bytes 12320768 | tf_op jit(solution)/shard_map/dot_general | solution.py:245
  420.0 0.0 collective-permute-done.5
  420.0 8.1 %multiply_convert_fusion.1 = bf16[1280,1024]{1,0:T(8,128)(2,1)} fusion(f32[1280,1024]{1,0:T(8,128)} %fusion.9, bf16[1536,1280]{1,0:T(8,128)(2,1)S(1)} %bitcast.32, bf16[768,1024]{1,0:T(8,128)(2,1)S(1)} %collective-permute-done.5, bf16[768,1024]{1,0:T(8,128)(2,1)} %collective-permute-done.4), kind=kOutput, calls=%fused_computation.2 | convolution fusion | flops 4036755456 | bytes 14942208 | tf_op jit(solution)/shard_map/dot_general | solution.py:248
  428.1 7.3 %multiply_convert_fusion.2 = bf16[1280,1024]{1,0:T(8,128)(2,1)} fusion(f32[1280,1024]{1,0:T(8,128)S(1)} %bitcast.45, bf16[1536,1280]{1,0:T(8,128)(2,1)S(1)} %bitcast.33, bf16[768,1024]{1,0:T(8,128)(2,1)S(1)} %collective-permute-done.2, bf16[768,1024]{1,0:T(8,128)(2,1)} %collective-permute-done.1), kind=kOutput, calls=%fused_computation.3 | convolution fusion | flops 4036755456 | bytes 14942208 | tf_op jit(solution)/shard_map/dot_general | solution.py:248
  435.5 6.1 %multiply_convert_fusion = bf16[1024,1280]{1,0:T(8,128)(2,1)} fusion(f32[1024,1280]{1,0:T(8,128)S(1)} %bitcast.43, bf16[1536,1280]{1,0:T(8,128)(2,1)S(1)} %bitcast.31, bf16[768,1024]{1,0:T(8,128)(2,1)S(1)} %collective-permute-done.8, bf16[768,1024]{1,0:T(8,128)(2,1)S(1)} %collective-permute-done.7), kind=kOutput, calls=%fused_computation.1 | convolution fusion | flops 4036755456 | bytes 14942208 | tf_op jit(solution)/shard_map/dot_general | solution.py:248
  (17 shorter events, 0.0 us)
Async XLA Ops:
  7.2 434.3 %reduce-scatter.2.cloned.1.call-start = ((), (), s32[]{:S(2)}) async-start(), calls=%async_computation.1 | async-start | bytes 8847360 | tf_op jit(solution)/shard_map/reduce_scatter | solution.py:225
  293.4 37.2 %collective-permute-start.7 = (bf16[768,1024]{1,0:T(8,128)(2,1)S(1)}, bf16[768,1024]{1,0:T(8,128)(2,1)S(1)}, u32[]{:S(2)}, u32[]{:S(2)}) collective-permute-start(bf16[768,1024]{1,0:T(8,128)(2,1)S(1)} %get-tuple-element.16), channel_id=1, source_target_pairs={{0,16},{8,24},{16,0},{24,8},{1,17},{9,25},{17,1},{25,9},{2,18},{10... | collective-permute-start | bytes 4718600 | tf_op jit(solution)/shard_map/ppermute | solution.py:239
  293.6 37.1 %collective-permute-start.3 = (bf16[768,1024]{1,0:T(8,128)(2,1)}, bf16[768,1024]{1,0:T(8,128)(2,1)}, u32[]{:S(2)}, u32[]{:S(2)}) collective-permute-start(bf16[768,1024]{1,0:T(8,128)(2,1)} %get-tuple-element.18), channel_id=1, source_target_pairs={{0,8},{8,0},{16,24},{24,16},{1,9},{9,1},{17,25},{25,17},{2,10},{10... | collective-permute-start | bytes 4718600 | tf_op jit(solution)/shard_map/ppermute | solution.py:240
  295.5 69.0 %collective-permute-start.4 = (bf16[768,1024]{1,0:T(8,128)(2,1)}, bf16[768,1024]{1,0:T(8,128)(2,1)}, u32[]{:S(2)}, u32[]{:S(2)}) collective-permute-start(bf16[768,1024]{1,0:T(8,128)(2,1)} %get-tuple-element.18), channel_id=1, source_target_pairs={{0,16},{8,24},{16,0},{24,8},{1,17},{9,25},{17,1},{25,9},{2,18},{10... | collective-permute-start | bytes 4718600 | tf_op jit(solution)/shard_map/ppermute | solution.py:239
  295.9 102.0 %collective-permute-start.1 = (bf16[768,1024]{1,0:T(8,128)(2,1)S(1)}, bf16[768,1024]{1,0:T(8,128)(2,1)}, u32[]{:S(2)}, u32[]{:S(2)}) collective-permute-start(bf16[768,1024]{1,0:T(8,128)(2,1)S(1)} %get-tuple-element.17), channel_id=1, source_target_pairs={{0,16},{8,24},{16,0},{24,8},{1,17},{9,25},{17,1},{25,9},{2,18},{10... | collective-permute-start | bytes 4718600 | tf_op jit(solution)/shard_map/ppermute | solution.py:239
  297.5 108.7 %collective-permute-start = (bf16[768,1024]{1,0:T(8,128)(2,1)S(1)}, bf16[768,1024]{1,0:T(8,128)(2,1)}, u32[]{:S(2)}, u32[]{:S(2)}) collective-permute-start(bf16[768,1024]{1,0:T(8,128)(2,1)S(1)} %get-tuple-element.17), channel_id=1, source_target_pairs={{0,8},{8,0},{16,24},{24,16},{1,9},{9,1},{17,25},{25,17},{2,10},{10... | collective-permute-start | bytes 4718600 | tf_op jit(solution)/shard_map/ppermute | solution.py:240
  330.7 83.1 %collective-permute-start.6 = (bf16[768,1024]{1,0:T(8,128)(2,1)S(1)}, bf16[768,1024]{1,0:T(8,128)(2,1)S(1)}, u32[]{:S(2)}, u32[]{:S(2)}) collective-permute-start(bf16[768,1024]{1,0:T(8,128)(2,1)S(1)} %get-tuple-element.16), channel_id=1, source_target_pairs={{0,8},{8,0},{16,24},{24,16},{1,9},{9,1},{17,25},{25,17},{2,10},{10... | collective-permute-start | bytes 4718600 | tf_op jit(solution)/shard_map/ppermute | solution.py:240
  330.7 104.8 %collective-permute-start.8 = (bf16[768,1024]{1,0:T(8,128)(2,1)S(1)}, bf16[768,1024]{1,0:T(8,128)(2,1)S(1)}, u32[]{:S(2)}, u32[]{:S(2)}) collective-permute-start(bf16[768,1024]{1,0:T(8,128)(2,1)S(1)} %collective-permute-done.7), channel_id=1, source_target_pairs={{0,8},{8,0},{16,24},{24,16},{1,9},{9,1},{17,25},{25,17},{2,10},{10... | collective-permute-start | bytes 4718600 | tf_op jit(solution)/shard_map/ppermute | solution.py:240
  364.5 55.5 %collective-permute-start.5 = (bf16[768,1024]{1,0:T(8,128)(2,1)}, bf16[768,1024]{1,0:T(8,128)(2,1)S(1)}, u32[]{:S(2)}, u32[]{:S(2)}) collective-permute-start(bf16[768,1024]{1,0:T(8,128)(2,1)} %collective-permute-done.4), channel_id=1, source_target_pairs={{0,8},{8,0},{16,24},{24,16},{1,9},{9,1},{17,25},{25,17},{2,10},{10... | collective-permute-start | bytes 4718600 | tf_op jit(solution)/shard_map/ppermute | solution.py:240
  397.9 30.2 %collective-permute-start.2 = (bf16[768,1024]{1,0:T(8,128)(2,1)}, bf16[768,1024]{1,0:T(8,128)(2,1)S(1)}, u32[]{:S(2)}, u32[]{:S(2)}) collective-permute-start(bf16[768,1024]{1,0:T(8,128)(2,1)} %collective-permute-done.1), channel_id=1, source_target_pairs={{0,8},{8,0},{16,24},{24,16},{1,9},{9,1},{17,25},{25,17},{2,10},{10... | collective-permute-start | bytes 4718600 | tf_op jit(solution)/shard_map/ppermute | solution.py:240
  413.8 14.3 %slice-start.2 = ((s8[5242880]{0:T(1024)(128)(4,1)}), s8[1048576]{0:T(1024)(128)(4,1)S(1)}, s32[]{:S(2)}) async-start(s8[5242880]{0:T(1024)(128)(4,1)} %bitcast.44), calls=%async_computation.4 | async-start | bytes 2097152
  420.0 8.1 %slice-start.3 = ((s8[5242880]{0:T(1024)(128)(4,1)}), s8[4194304]{0:T(1024)(128)(4,1)S(1)}, s32[]{:S(2)}) async-start(s8[5242880]{0:T(1024)(128)(4,1)} %bitcast.44), calls=%async_computation.5 | async-start | bytes 8388608
  420.0 15.4 %slice-start = ((s8[5242880]{0:T(1024)(128)(4,1)}), s8[1048576]{0:T(1024)(128)(4,1)S(1)}, s32[]{:S(2)}) async-start(s8[5242880]{0:T(1024)(128)(4,1)} %bitcast.42), calls=%async_computation.2 | async-start | bytes 2097152
  428.1 7.3 %slice-start.1 = ((s8[5242880]{0:T(1024)(128)(4,1)}), s8[4194304]{0:T(1024)(128)(4,1)S(1)}, s32[]{:S(2)}) async-start(s8[5242880]{0:T(1024)(128)(4,1)} %bitcast.42), calls=%async_computation.3 | async-start | bytes 8388608
Sparse Core Ops, SparseCore 0:
  293.5 140.6 reduce-scatter.1

commit v2 on v1

--- a/solution.py
+++ b/solution.py
@@ -3,6 +3,7 @@
 
 import jax
 import jax.numpy as jnp
+import numpy as np
 from jax import lax
 from jax.experimental import pallas as pl
 from jax.experimental.pallas import tpu as pltpu
@@ -20,7 +21,9 @@
     return p
 
 
-def gather_kernel(n_tok, n_hid, x_ref, g_ref, xf, gf, xc, gc, local_sem, ag_send, ag_recv, col_send, col_recv):
+def gather_kernel(n_tok, n_hid, *refs):
+    x_ref, g_ref = refs[:2]
+    xf, gf, xc, gc, local_sem, ag_send, ag_recv, col_send, col_recv = refs[-9:]
     t = lax.axis_index("tok")
     h = lax.axis_index("hid")
     lines = n_hid // 2
@@ -153,7 +156,7 @@
                 col(a, fulls[a].at[s], s, j).wait_recv()
 
 
-def gather(layer_input, output_grad, n_tok, n_hid):
+def gather(layer_input, output_grad, n_tok, n_hid, call, after):
     rows, depth = layer_input.shape
     width = depth // n_tok
     full = jax.ShapeDtypeStruct((n_hid, rows, depth), jnp.bfloat16)
@@ -162,7 +165,7 @@
     return pl.pallas_call(
         functools.partial(gather_kernel, n_tok, n_hid),
         out_shape=(full, full, cols, cols),
-        in_specs=[anywhere] * 2,
+        in_specs=[anywhere] * (2 + len(after)),
         out_specs=(anywhere,) * 4,
         scratch_shapes=[
             pltpu.SemaphoreType.DMA((2, n_hid + 1)),
@@ -171,9 +174,22 @@
             pltpu.SemaphoreType.DMA((2, n_tok, n_hid)),
             pltpu.SemaphoreType.DMA((2, n_tok, n_hid)),
         ],
-        compiler_params=pltpu.CompilerParams(collective_id=0, has_side_effects=True),
-        name="gather_rows_and_columns",
-    )(layer_input, output_grad)
+        compiler_params=pltpu.CompilerParams(collective_id=call, has_side_effects=True),
+        cost_estimate=pl.CostEstimate(flops=0, bytes_accessed=rows * n_hid * depth * 40, transcendentals=0),
+        name="gather_rows_and_columns_%d" % call,
+    )(layer_input, output_grad, *after)
+
+
+def hold_until(values, after):
+    anywhere = pl.BlockSpec(memory_space=pl.ANY)
+    return pl.pallas_call(
+        lambda *refs: None,
+        out_shape=[jax.ShapeDtypeStruct(v.shape, v.dtype) for v in values],
+        in_specs=[anywhere] * (len(values) + len(after)),
+        out_specs=[anywhere] * len(values),
+        input_output_aliases={i: i for i in range(len(values))},
+        name="hold_until",
+    )(*values, *after)
 
 
 def unit_grads(gate_pre, up_pre, grad_hidden, unit_mask):
@@ -198,61 +214,74 @@
     contract_first = (((0,), (0,)), ((), ()))
     n_tok, n_hid = lax.axis_size("tok"), lax.axis_size("hid")
     width = gate_weight.shape[1]
-    depth = layer_input.shape[1]
-    tok_rows = layer_input.shape[0] * n_hid
+    rows, depth = layer_input.shape
+    tok_rows = rows * n_hid
     blocks_here = width // BLOCK
     local_blocks = lax.axis_index("hid") * blocks_here + jnp.arange(blocks_here, dtype=jnp.int32)
-    active = tile_activity(block_lists, block_count, local_blocks)
-    inputs_full, grads_full, inputs_cols, grads_cols = gather(layer_input, output_grad, n_tok, n_hid)
-    inputs_full = inputs_full.reshape(tok_rows, depth)
-    grads_full = grads_full.reshape(tok_rows, depth)
-    inputs_cols = inputs_cols.reshape(n_tok * tok_rows, depth // n_tok)
-    grads_cols = grads_cols.reshape(n_tok * tok_rows, depth // n_tok)
-    tiles_here = tok_rows // TILE
-    unit_mask = jnp.broadcast_to(
-        active.astype(jnp.float32)[:, None, :, None], (tiles_here, TILE, blocks_here, BLOCK)
-    ).reshape(tok_rows, width)
-    gate_pre = jnp.dot(inputs_full, gate_weight, preferred_element_type=jnp.float32)
-    up_pre = jnp.dot(inputs_full, up_weight, preferred_element_type=jnp.float32)
-    grad_hidden = lax.dot_general(
-        grads_full, down_weight, contract_last, preferred_element_type=jnp.float32
+    active = tile_activity(block_lists, block_count, local_blocks).astype(jnp.float32)
+    over_core = [(i, i + 1 - 2 * (i % 2)) for i in range(n_tok)]
+    scale = 1.0 / math.sqrt(tok_rows * n_tok)
+
+    def front(x, g, first_row, call, start_after=(), use_after=()):
+        n = x.shape[0]
+        x_full, g_full, x_cols, g_cols = gather(x, g, n_tok, n_hid, call, start_after)
+        if use_after:
+            x_full, g_full = hold_until((x_full, g_full), use_after)
+        x_full, g_full = x_full.reshape(n * n_hid, depth), g_full.reshape(n * n_hid, depth)
+        tiles = (np.arange(n_hid)[:, None] * rows + first_row + np.arange(n)[None, :]).reshape(-1) // TILE
+        pick = jnp.asarray(tiles)[:, None] == jnp.arange(active.shape[0])[None, :]
+        row_active = jnp.dot(pick.astype(jnp.float32), active)
+        unit_mask = jnp.broadcast_to(row_active[:, :, None], (n * n_hid, blocks_here, BLOCK)).reshape(-1, width)
+        gate_pre = jnp.dot(x_full, gate_weight, preferred_element_type=jnp.float32)
+        up_pre = jnp.dot(x_full, up_weight, preferred_element_type=jnp.float32)
+        grad_hidden = lax.dot_general(g_full, down_weight, contract_last, preferred_element_type=jnp.float32)
+        acts = unit_grads(gate_pre, up_pre, grad_hidden, unit_mask)
+        return acts, x_cols.reshape(-1, x_cols.shape[-1]), g_cols.reshape(-1, g_cols.shape[-1])
+
+    def input_partial(acts):
+        _, grad_gate, grad_up = acts
+        total = lax.dot_general(grad_gate, gate_weight, contract_last, preferred_element_type=jnp.float32)
+        return (
+            total + lax.dot_general(grad_up, up_weight, contract_last, preferred_element_type=jnp.float32)
+        ).astype(jnp.bfloat16)
+
+    def cross(acts):
+        far = [[(d, (d + 2 * k) % n_tok) for d in range(n_tok)] for k in range(1, n_tok // 2)]
+        return [[lax.ppermute(arr, "tok", perm) for perm in far] for arr in acts]
+
+    def spread(acts, crossed):
+        slots = []
+        for arr, others in zip(acts, crossed):
+            parts = []
+            for one in [arr] + others:
+                parts += [one, lax.ppermute(one, "tok", over_core)]
+            slots.append(jnp.concatenate(parts))
+        return slots
+
+    def scatter(partial):
+        return lax.psum_scatter(partial, "hid", scatter_dimension=0, tiled=True)
+
+    cut = rows * 2 // 3
+    acts0, x_cols0, g_cols0 = front(layer_input[:cut], output_grad[:cut], 0, 0)
+    crossed0 = cross(acts0)
+    partial0 = input_partial(acts0)
+    input_grad0 = scatter(partial0)
+    acts1, x_cols1, g_cols1 = front(
+        layer_input[cut:], output_grad[cut:], cut, 1, (partial0,), (input_grad0, *sum(crossed0, []))
     )
-    acts = unit_grads(gate_pre, up_pre, grad_hidden, unit_mask)
-    _, grad_gate, grad_up = acts
-    total = lax.dot_general(
-        grad_gate, gate_weight, contract_last, preferred_element_type=jnp.float32
-    )
-    input_grad = lax.psum_scatter(
-        (
-            total
-            + lax.dot_general(grad_up, up_weight, contract_last, preferred_element_type=jnp.float32)
-        ).astype(jnp.bfloat16),
-        "hid",
-        scatter_dimension=0,
-        tiled=True,
-    )
-    over_core = [(i, i + 1 - 2 * (i % 2)) for i in range(n_tok)]
-    slots = [[], [], []]
-    for k in range(n_tok // 2):
-        for i, arr in enumerate(acts):
-            if k:
-                arr = lax.ppermute(arr, "tok", [(d, (d + 2 * k) % n_tok) for d in range(n_tok)])
-            slots[i] += [arr, lax.ppermute(arr, "tok", over_core)]
-    scale = 1.0 / math.sqrt(tok_rows * n_tok)
-    near = 2 * tok_rows
-
-    def weight_sum(columns, parts):
-        first = lax.dot_general(
-            columns[:near], jnp.concatenate(parts[:2]), contract_first, preferred_element_type=jnp.float32
-        )
-        rest = lax.dot_general(
-            columns[near:], jnp.concatenate(parts[2:]), contract_first, preferred_element_type=jnp.float32
-        )
-        return (first + rest) * scale
-
-    gate_grad = weight_sum(inputs_cols, slots[1]).astype(jnp.bfloat16)
-    up_grad = weight_sum(inputs_cols, slots[2]).astype(jnp.bfloat16)
-    down_grad = weight_sum(grads_cols, slots[0]).T.astype(jnp.bfloat16)
+    crossed1 = cross(acts1)
+    input_grad = jnp.concatenate([input_grad0, scatter(input_partial(acts1))])
+    all0, all1 = spread(acts0, crossed0), spread(acts1, crossed1)
+
+    def weight_sum(cols0, cols1, i):
+        return (
+            lax.dot_general(cols0, all0[i], contract_first, preferred_element_type=jnp.float32)
+            + lax.dot_general(cols1, all1[i], contract_first, preferred_element_type=jnp.float32)
+        ) * scale
+
+    gate_grad = weight_sum(x_cols0, x_cols1, 1).astype(jnp.bfloat16)
+    up_grad = weight_sum(x_cols0, x_cols1, 2).astype(jnp.bfloat16)
+    down_grad = weight_sum(g_cols0, g_cols1, 0).T.astype(jnp.bfloat16)
     return (input_grad, gate_grad, up_grad, down_grad)
 
 

time: 449 us -> 483 us (1.076); the launches traced: 448 us -> 474 us
  Pallas kernels: 210 us -> 265 us
  waiting for transfers between devices: 92.9 us -> 43.8 us
  matrix products: 118 us -> 129 us
  starting transfers between devices: 4.69 us -> 10.4 us
    ppermute x9 -> x18, waiting for transfers between devices: 92.9 us -> 24.2 us  [the longest x6 24.1 us: cross(): return [[lax.ppermute(arr, 'tok', perm) for perm in far] for arr in acts]]
    pallas_call x1 -> x2, Pallas kernels: 210 us -> 265 us  [gather(): pl.pallas_call(functools.partial(gather_kernel, n_tok, n_hid), out_shape=...]
    reduce_scatter x1 -> x2, waiting for transfers between devices: 0.01 us -> 19.6 us  [scatter(): return lax.psum_scatter(partial, 'hid', scatter_dimension=0, tiled=True)]
    dot_general x11 -> x18, matrix products: 118 us -> 129 us  [the longest x3 26.4 us: weight_sum(): lax.dot_general(cols0, all0[i], contract_first, preferred_element_type=jn...]
    ppermute x9 -> x18, starting transfers between devices: 4.65 us -> 10.3 us  [the longest x6 7.25 us: cross(): return [[lax.ppermute(arr, 'tok', perm) for perm in far] for arr in acts]]
  transfers between devices with their start and end apart: 10 -> 20, of which waited for: 3 -> 5; matrix products, arithmetic and copies ran while one was open for 11% -> 17% of each run, Pallas kernels for 0% -> 26%
where the time goes in v2:
time: 483 us; the launch traced here: 474 us
  Pallas kernels  265 us (55%)
  matrix products  129 us (27%)
  waiting for transfers between devices  43.8 us (9%)
  between operations  14.9 us (3%)
  starting transfers between devices  10.4 us (2%)
  local copies, waits for them, and re-layouts  8.4 us (2%)
    pallas_call x2, Pallas kernels, gather(): pl.pallas_call(functools.partial(gather_kernel, n_tok, n_hid), out_shape=...  265 us
    dot_general x3, matrix products, weight_sum(): lax.dot_general(cols0, all0[i], contract_first, preferred_element_type=jn...  26.4 us
    ppermute x6, waiting for transfers between devices, cross(): return [[lax.ppermute(arr, 'tok', perm) for perm in far] for arr in acts]  24.1 us
    dot_general x2, matrix products, front(): up_pre = jnp.dot(x_full, up_weight, preferred_element_type=jnp.float32)  21.5 us
    dot_general x2, matrix products, input_partial(): lax.dot_general(grad_up, up_weight, contract_last, preferred_element_type...  20.5 us
    dot_general x2, matrix products, front(): gate_pre = jnp.dot(x_full, gate_weight, preferred_element_type=jnp.float32)  19.7 us
    reduce_scatter x2, waiting for transfers between devices, scatter(): return lax.psum_scatter(partial, 'hid', scatter_dimension=0, tiled=True)  19.6 us
    dot_general x2, matrix products, front(): lax.dot_general(g_full, down_weight, contract_last, preferred_element_typ...  15 us
  transfers between devices with their start and end apart: 20, of which 5 were waited for; matrix products, arithmetic and copies ran while one was open for 17% of the time, Pallas kernels for 26%

profile of v2, /device:TPU:0, one launch (start us, length us, event | category | flops | bytes accessed | tf_op | source)
XLA Modules:
  0.0 474.5 jit_solution(14488207219365789778)
XLA Ops:
  7.2 2.0 slice.12.refs_0_
  9.2 2.0 slice.13.refs_1_
  11.9 143.1 %gather_rows_and_columns_0.1 = (bf16[8,64,5120]{2,1,0:T(8,128)(2,1)}, bf16[8,64,5120]{2,1,0:T(8,128)(2,1)}, bf16[4,8,64,1280]{3,2,1,0:T(8,128)(2,1)}, bf16[4,8,64,1280]{3,2,1,0:T(8,128)(2,1)}) custom-call(bf16[64,5120]{1,0:T(8,128)(2,1)} %slice.12.refs_0_, bf16[64,5120]{1,0:T(8,128)(2,1)} %slice.13.refs_1_), custom_call_target="tpu_custom_call" | custom-call | bytes 104857600 | tf_op jit(solution)/shard_map/gather_rows_and_columns_0/pallas_call | solution.py:165
  156.9 10.9 %fusion.62 = f32[512,1024]{1,0:T(8,128)} fusion(bf16[512,5120]{1,0:T(8,128)(2,1)} %bitcast.70, bf16[5120,1024]{1,0:T(8,128)(2,1)} %param.11), kind=kOutput, calls=%fused_computation.83 | convolution fusion | flops 5368709120 | bytes 17825792 | tf_op jit(solution)/shard_map/dot_general | solution.py:235
  168.5 8.8 %bitcast_multiply_fusion.1 = f32[512,1024]{1,0:T(8,128)} fusion(f32[64,8,8,128]{3,2,1,0:T(8,128)S(1)} %bitcast.55, bf16[512,5120]{1,0:T(8,128)(2,1)} %bitcast.72, bf16[1024,5120]{1,0:T(8,128)(2,1)S(1)} %bitcast.60), kind=kOutput, calls=%fused_computation.28 | convolution fusion | flops 5369233408 | bytes 19922944 | tf_op jit(solution)/shard_map/dot_general | solution.py:237
  177.2 12.7 %fusion.23 = (bf16[512,1024]{1,0:T(8,128)(2,1)}, bf16[512,1024]{1,0:T(8,128)(2,1)S(1)}, bf16[512,1024]{1,0:T(8,128)(2,1)}) fusion(f32[64,8,8,128]{3,2,1,0:T(8,128)S(1)} %bitcast.56, f32[512,1024]{1,0:T(8,128)} %fusion.62, f32[512,1024]{1,0:T(8,128)} %bitcast_multiply_fusion.1, bf16[512,5120]{1,0:T(8,128)(2,1)} %bitcast.71, bf16[5120,1024]{1,0:T(8,128)(2,1)} %param.12), kind=kOutput, calls=%fused_computation.30 | convolution fusion | flops 5377097728 | bytes 25165824 | tf_op jit(solution)/shard_map/dot_general | solution.py:236
  189.9 8.8 %fusion.63 = f32[512,5120]{1,0:T(8,128)S(1)} fusion(bf16[512,1024]{1,0:T(8,128)(2,1)S(1)} %get-tuple-element.25, bf16[5120,1024]{1,0:T(8,128)(2,1)} %param.11), kind=kOutput, calls=%fused_computation.84 | convolution fusion | flops 5368709120 | bytes 22020096 | tf_op jit(solution)/shard_map/dot_general | solution.py:243
  198.8 10.4 %add_convert_fusion.refs_2_ = bf16[512,5120]{1,0:T(8,128)(2,1)} fusion(f32[512,5120]{1,0:T(8,128)S(1)} %fusion.63, bf16[512,1024]{1,0:T(8,128)(2,1)} %get-tuple-element.26, bf16[5120,1024]{1,0:T(8,128)(2,1)} %param.12), kind=kOutput, calls=%fused_computation | convolution fusion | flops 5373952000 | bytes 27262976 | tf_op jit(solution)/shard_map/dot_general | solution.py:245
  210.0 1.3 collective-permute-start.1
  212.8 1.7 slice.14.refs_0_
  214.5 1.7 slice.15.refs_1_
  216.2 121.7 %gather_rows_and_columns_1.1 = (bf16[8,32,5120]{2,1,0:T(8,128)(2,1)}, bf16[8,32,5120]{2,1,0:T(8,128)(2,1)}, bf16[4,8,32,1280]{3,2,1,0:T(8,128)(2,1)}, bf16[4,8,32,1280]{3,2,1,0:T(8,128)(2,1)}) custom-call(bf16[32,5120]{1,0:T(8,128)(2,1)} %slice.14.refs_0_, bf16[32,5120]{1,0:T(8,128)(2,1)} %slice.15.refs_1_, bf16[512,5120]{1,0:T(8,128)(2,1)} %add_convert_fusion.refs_2_), custom_call_target="tpu_custom_call" | custom-call | bytes 52428800 | tf_op jit(solution)/shard_map/gather_rows_and_columns_1/pallas_call | solution.py:165
  338.7 7.5 %reduce-scatter.3.cloned.1.call-done.refs_2_ = bf16[64,5120]{1,0:T(8,128)(2,1)} async-done(((bf16[512,5120]{1,0:T(8,128)(2,1)}), bf16[64,5120]{1,0:T(8,128)(2,1)}) %reduce-scatter.3.cloned.1.call-update) | async-done | bytes 655376 | tf_op jit(solution)/shard_map/reduce_scatter | solution.py:262
  346.2 8.8 %fusion.64 = f32[256,1024]{1,0:T(8,128)} fusion(bf16[256,5120]{1,0:T(8,128)(2,1)} %bitcast.52, bf16[5120,1024]{1,0:T(8,128)(2,1)} %param.11), kind=kOutput, calls=%fused_computation.85 | convolution fusion | flops 2684354560 | bytes 14155776 | tf_op jit(solution)/shard_map/dot_general | solution.py:235
  355.3 6.2 %convolution_multiply_fusion = f32[256,1024]{1,0:T(8,128)S(1)} fusion(bf16[256,5120]{1,0:T(8,128)(2,1)S(1)} %bitcast.54, bf16[1024,5120]{1,0:T(8,128)(2,1)} %param.13, f32[32,8,8,128]{3,2,1,0:T(8,128)S(1)} %bitcast.57), kind=kOutput, calls=%fused_computation.59 | convolution fusion | flops 2684616704 | bytes 15204352 | tf_op jit(solution)/shard_map/dot_general | solution.py:237
  361.5 8.8 %fusion.50 = (bf16[256,1024]{1,0:T(8,128)(2,1)}, bf16[256,1024]{1,0:T(8,128)(2,1)S(1)}, bf16[256,1024]{1,0:T(8,128)(2,1)}) fusion(f32[32,8,8,128]{3,2,1,0:T(8,128)S(1)} %bitcast.58, f32[256,1024]{1,0:T(8,128)} %fusion.64, f32[256,1024]{1,0:T(8,128)S(1)} %convolution_multiply_fusion, bf16[256,5120]{1,0:T(8,128)(2,1)S(1)} %bitcast.53, ...), kind=kOutput, calls=%fused_computation.62 | convolution fusion | flops 2688548864 | bytes 17825792 | tf_op jit(solution)/shard_map/dot_general | solution.py:236
  370.3 1.5 collective-permute-start.11
  371.8 4.7 fusion.65
  376.5 7.7 %collective-permute-done.11 = bf16[256,1024]{1,0:T(8,128)(2,1)} collective-permute-done((bf16[256,1024]{1,0:T(8,128)(2,1)}, bf16[256,1024]{1,0:T(8,128)(2,1)}, u32[]{:S(2)}, u32[]{:S(2)}) %collective-permute-start.11) | collective-permute-done | bytes 524320 | tf_op jit(solution)/shard_map/ppermute | solution.py:250
  384.2 10.1 %fusion = bf16[256,5120]{1,0:T(8,128)(2,1)} fusion(f32[256,5120]{1,0:T(8,128)} %fusion.65, bf16[256,1024]{1,0:T(8,128)(2,1)} %get-tuple-element.29, bf16[5120,1024]{1,0:T(8,128)(2,1)} %param.12), kind=kOutput, calls=%fused_computation.2 | convolution fusion | flops 2686976000 | bytes 18874368 | tf_op jit(solution)/shard_map/dot_general | solution.py:245
  394.9 1.5 collective-permute-start.16
  396.3 4.9 %fusion.32 = f32[1280,1024]{1,0:T(8,128)S(1)} fusion(bf16[1024,1280]{1,0:T(8,128)(2,1)S(1)} %bitcast.73, bf16[256,1024]{1,0:T(8,128)(2,1)} %collective-permute-done.12, bf16[256,1024]{1,0:T(8,128)(2,1)} %collective-permute-done.11, bf16[256,1024]{1,0:T(8,128)(2,1)} %collective-permute-done.10, bf16[256,1024]{1,0:T(8,128)(2,1)} %get-tuple-element.29), kind=kOutput, calls=%fused_computation.39 | convolution fusion | flops 2692743168 | bytes 9961472 | tf_op jit(solution)/shard_map/dot_general | solution.py:279
  401.8 7.1 %collective-permute-done.16 = bf16[256,1024]{1,0:T(8,128)(2,1)S(1)} collective-permute-done((bf16[256,1024]{1,0:T(8,128)(2,1)}, bf16[256,1024]{1,0:T(8,128)(2,1)S(1)}, u32[]{:S(2)}, u32[]{:S(2)}) %collective-permute-start.16) | collective-permute-done | bytes 524320 | tf_op jit(solution)/shard_map/ppermute | solution.py:250
  409.0 10.7 %multiply_convert_fusion.1 = bf16[1280,1024]{1,0:T(8,128)(2,1)} fusion(f32[1280,1024]{1,0:T(8,128)S(1)} %fusion.32, bf16[2048,1280]{1,0:T(8,128)(2,1)} %bitcast.63, bf16[512,1024]{1,0:T(8,128)(2,1)} %collective-permute-done.9, bf16[512,1024]{1,0:T(8,128)(2,1)} %collective-permute-done.2.refs_5_, bf16[512,1024]{1,0:T(8,128)(2,1)} %collective-permute-done.8, ...), kind=kOutput, calls=%fused_computation.4 | convolution fusion | flops 5389418496 | bytes 17301504 | tf_op jit(solution)/shard_map/dot_general | solution.py:278
  420.3 1.5 collective-permute-start.6
  421.8 3.0 fusion.40
  424.9 9.3 %collective-permute-done.6 = bf16[256,1024]{1,0:T(8,128)(2,1)S(1)} collective-permute-done((bf16[256,1024]{1,0:T(8,128)(2,1)S(1)}, bf16[256,1024]{1,0:T(8,128)(2,1)S(1)}, u32[]{:S(2)}, u32[]{:S(2)}) %collective-permute-start.6) | collective-permute-done | bytes 524320 | tf_op jit(solution)/shard_map/ppermute | solution.py:250
  434.3 8.6 %multiply_convert_fusion = bf16[1024,1280]{1,0:T(8,128)(2,1)} fusion(f32[1024,1280]{1,0:T(8,128)S(1)} %fusion.40, bf16[2048,1280]{1,0:T(8,128)(2,1)S(1)} %bitcast.69, bf16[512,1024]{1,0:T(8,128)(2,1)S(1)} %collective-permute-done.14, bf16[512,1024]{1,0:T(8,128)(2,1)S(1)} %copy-done.6, bf16[512,1024]{1,0:T(8,128)(2,1)} %collective-permute-done.13, ...), kind=kOutput, calls=%fused_computation.3 | convolution fusion | flops 5389418496 | bytes 17301504 | tf_op jit(solution)/shard_map/dot_general | solution.py:278
  442.9 2.9 fusion.24
  445.9 7.1 %multiply_convert_fusion.2 = bf16[1280,1024]{1,0:T(8,128)(2,1)} fusion(f32[1280,1024]{1,0:T(8,128)S(1)} %fusion.24, bf16[2048,1280]{1,0:T(8,128)(2,1)S(1)} %bitcast.66, bf16[512,1024]{1,0:T(8,128)(2,1)S(1)} %collective-permute-done.4, bf16[512,1024]{1,0:T(8,128)(2,1)S(1)} %copy-done.4, bf16[512,1024]{1,0:T(8,128)(2,1)S(1)} %collective-permute-done.3, ...), kind=kOutput, calls=%fused_computation.5 | convolution fusion | flops 5389418496 | bytes 17301504 | tf_op jit(solution)/shard_map/dot_general | solution.py:278
  453.0 12.1 %reduce-scatter.5.cloned.1.call-done = bf16[32,5120]{1,0:T(8,128)(2,1)} async-done(((bf16[256,5120]{1,0:T(8,128)(2,1)}), bf16[32,5120]{1,0:T(8,128)(2,1)}) %reduce-scatter.5.cloned.1.call-update) | async-done | bytes 327696 | tf_op jit(solution)/shard_map/reduce_scatter | solution.py:262
  465.2 2.0 pad_maximum_fusion
  (93 shorter events, 8.6 us)
Async XLA Ops:
  7.2 339.0 %reduce-scatter.3.cloned.1.call-start = ((), (), s32[]{:S(2)}) async-start(), calls=%async_computation.2 | async-start | bytes 5898240 | tf_op jit(solution)/shard_map/reduce_scatter | solution.py:262
  11.9 156.6 %slice-start = ((s8[10485760]{0:T(1024)(128)(4,1)}), s8[2097152]{0:T(1024)(128)(4,1)S(1)}, s32[]{:S(2)}) async-start(s8[10485760]{0:T(1024)(128)(4,1)} %bitcast.59), calls=%async_computation.4 | async-start | bytes 4194304
  189.9 20.1 %copy-start.10 = (bf16[512,1024]{1,0:T(8,128)(2,1)}, bf16[512,1024]{1,0:T(8,128)(2,1)S(1)}, u32[]{:S(2)}) copy-start(bf16[512,1024]{1,0:T(8,128)(2,1)S(1)} %get-tuple-element.25) | copy-start | bytes 3145732
  209.2 128.7 %copy-start.7 = (s32[256]{0:T(256)S(1)}, s32[256]{0:T(256)}, u32[]{:S(2)}) copy-start(s32[256]{0:T(256)} %constant.18.clone) | copy-start | bytes 3076
  209.2 255.9 %reduce-scatter.5.cloned.1.call-start = ((), (), s32[]{:S(2)}) async-start(), calls=%async_computation.3 | async-start | bytes 2949120 | tf_op jit(solution)/shard_map/reduce_scatter | solution.py:262
  209.3 128.9 %collective-permute-start.2 = (bf16[512,1024]{1,0:T(8,128)(2,1)}, bf16[512,1024]{1,0:T(8,128)(2,1)}, u32[]{:S(2)}, u32[]{:S(2)}) collective-permute-start(bf16[512,1024]{1,0:T(8,128)(2,1)} %get-tuple-element.26), channel_id=1, source_target_pairs={{0,16},{8,24},{16,0},{24,8},{1,17},{9,25},{17,1},{25,9},{2,18},{10... | collective-permute-start | bytes 3145736 | tf_op jit(solution)/shard_map/ppermute | solution.py:250
  210.0 128.6 %collective-permute-start.1 = (bf16[512,1024]{1,0:T(8,128)(2,1)S(1)}, bf16[512,1024]{1,0:T(8,128)(2,1)S(1)}, u32[]{:S(2)}, u32[]{:S(2)}) collective-permute-start(bf16[512,1024]{1,0:T(8,128)(2,1)S(1)} %get-tuple-element.25), channel_id=1, source_target_pairs={{0,16},{8,24},{16,0},{24,8},{1,17},{9,25},{17,1},{25,9},{2,18},{10... | collective-permute-start | bytes 3145736 | tf_op jit(solution)/shard_map/ppermute | solution.py:250
  211.3 127.3 %collective-permute-start = (bf16[512,1024]{1,0:T(8,128)(2,1)}, bf16[512,1024]{1,0:T(8,128)(2,1)S(1)}, u32[]{:S(2)}, u32[]{:S(2)}) collective-permute-start(bf16[512,1024]{1,0:T(8,128)(2,1)} %get-tuple-element.24), channel_id=1, source_target_pairs={{0,16},{8,24},{16,0},{24,8},{1,17},{9,25},{17,1},{25,9},{2,18},{10... | collective-permute-start | bytes 3145736 | tf_op jit(solution)/shard_map/ppermute | solution.py:250
  212.1 212.8 %collective-permute-start.13 = (bf16[512,1024]{1,0:T(8,128)(2,1)}, bf16[512,1024]{1,0:T(8,128)(2,1)}, u32[]{:S(2)}, u32[]{:S(2)}) collective-permute-start(bf16[512,1024]{1,0:T(8,128)(2,1)} %get-tuple-element.24), channel_id=1, source_target_pairs={{0,8},{8,0},{16,24},{24,16},{1,9},{9,1},{17,25},{25,17},{2,10},{10... | collective-permute-start | bytes 3145736 | tf_op jit(solution)/shard_map/ppermute | solution.py:257
  212.8 188.5 %collective-permute-start.8 = (bf16[512,1024]{1,0:T(8,128)(2,1)}, bf16[512,1024]{1,0:T(8,128)(2,1)}, u32[]{:S(2)}, u32[]{:S(2)}) collective-permute-start(bf16[512,1024]{1,0:T(8,128)(2,1)} %get-tuple-element.26), channel_id=1, source_target_pairs={{0,8},{8,0},{16,24},{24,16},{1,9},{9,1},{17,25},{25,17},{2,10},{10... | collective-permute-start | bytes 3145736 | tf_op jit(solution)/shard_map/ppermute | solution.py:257
  338.1 63.2 %collective-permute-start.9 = (bf16[512,1024]{1,0:T(8,128)(2,1)}, bf16[512,1024]{1,0:T(8,128)(2,1)}, u32[]{:S(2)}, u32[]{:S(2)}) collective-permute-start(bf16[512,1024]{1,0:T(8,128)(2,1)} %collective-permute-done.2.refs_5_), channel_id=1, source_target_pairs={{0,8},{8,0},{16,24},{24,16},{1,9},{9,1},{17,25},{25,17},{2,10},{10... | collective-permute-start | bytes 3145736 | tf_op jit(solution)/shard_map/ppermute | solution.py:257
  355.3 16.5 %slice-start.3 = ((s8[10485760]{0:T(1024)(128)(4,1)}), s8[4194304]{0:T(1024)(128)(4,1)S(1)}, s32[]{:S(2)}) async-start(s8[10485760]{0:T(1024)(128)(4,1)} %bitcast.61), calls=%async_computation.7 | async-start | bytes 8388608
  355.3 16.5 %slice-start.4 = ((s8[10485760]{0:T(1024)(128)(4,1)}), s8[4194304]{0:T(1024)(128)(4,1)S(1)}, s32[]{:S(2)}) async-start(s8[10485760]{0:T(1024)(128)(4,1)} %bitcast.61), calls=%async_computation.8 | async-start | bytes 8388608
  370.3 13.9 %collective-permute-start.11 = (bf16[256,1024]{1,0:T(8,128)(2,1)}, bf16[256,1024]{1,0:T(8,128)(2,1)}, u32[]{:S(2)}, u32[]{:S(2)}) collective-permute-start(bf16[256,1024]{1,0:T(8,128)(2,1)} %get-tuple-element.29), channel_id=1, source_target_pairs={{0,16},{8,24},{16,0},{24,8},{1,17},{9,25},{17,1},{25,9},{2,18},{10... | collective-permute-start | bytes 1572872 | tf_op jit(solution)/shard_map/ppermute | solution.py:250
  371.8 22.5 %collective-permute-start.10 = (bf16[256,1024]{1,0:T(8,128)(2,1)}, bf16[256,1024]{1,0:T(8,128)(2,1)}, u32[]{:S(2)}, u32[]{:S(2)}) collective-permute-start(bf16[256,1024]{1,0:T(8,128)(2,1)} %get-tuple-element.29), channel_id=1, source_target_pairs={{0,8},{8,0},{16,24},{24,16},{1,9},{9,1},{17,25},{25,17},{2,10},{10... | collective-permute-start | bytes 1572872 | tf_op jit(solution)/shard_map/ppermute | solution.py:257
  376.5 19.8 %copy-start.8 = (bf16[4,8,32,1280]{3,2,1,0:T(8,128)(2,1)S(1)}, bf16[4,8,32,1280]{3,2,1,0:T(8,128)(2,1)}, u32[]{:S(2)}) copy-start(bf16[4,8,32,1280]{3,2,1,0:T(8,128)(2,1)} %get-tuple-element.21) | copy-start | bytes 7864324
  384.2 10.7 %collective-permute-start.12 = (bf16[256,1024]{1,0:T(8,128)(2,1)}, bf16[256,1024]{1,0:T(8,128)(2,1)}, u32[]{:S(2)}, u32[]{:S(2)}) collective-permute-start(bf16[256,1024]{1,0:T(8,128)(2,1)} %collective-permute-done.11), channel_id=1, source_target_pairs={{0,8},{8,0},{16,24},{24,16},{1,9},{9,1},{17,25},{25,17},{2,10},{10... | collective-permute-start | bytes 1572872 | tf_op jit(solution)/shard_map/ppermute | solution.py:257
  394.3 51.6 %collective-permute-start.3 = (bf16[512,1024]{1,0:T(8,128)(2,1)}, bf16[512,1024]{1,0:T(8,128)(2,1)S(1)}, u32[]{:S(2)}, u32[]{:S(2)}) collective-permute-start(bf16[512,1024]{1,0:T(8,128)(2,1)} %copy-done.10), channel_id=1, source_target_pairs={{0,8},{8,0},{16,24},{24,16},{1,9},{9,1},{17,25},{25,17},{2,10},{10... | collective-permute-start | bytes 3145736 | tf_op jit(solution)/shard_map/ppermute | solution.py:257
  394.9 14.1 %collective-permute-start.16 = (bf16[256,1024]{1,0:T(8,128)(2,1)}, bf16[256,1024]{1,0:T(8,128)(2,1)S(1)}, u32[]{:S(2)}, u32[]{:S(2)}) collective-permute-start(bf16[256,1024]{1,0:T(8,128)(2,1)} %get-tuple-element.27), channel_id=1, source_target_pairs={{0,16},{8,24},{16,0},{24,8},{1,17},{9,25},{17,1},{25,9},{2,18},{10... | collective-permute-start | bytes 1572872 | tf_op jit(solution)/shard_map/ppermute | solution.py:250
  396.3 37.9 %slice-start.8 = ((s8[5242880]{0:T(1024)(128)(4,1)}), s8[4194304]{0:T(1024)(128)(4,1)S(1)}, s32[]{:S(2)}) async-start(s8[5242880]{0:T(1024)(128)(4,1)} %bitcast.67), calls=%async_computation.12 | async-start | bytes 8388608
  401.3 33.0 %collective-permute-start.14 = (bf16[512,1024]{1,0:T(8,128)(2,1)S(1)}, bf16[512,1024]{1,0:T(8,128)(2,1)S(1)}, u32[]{:S(2)}, u32[]{:S(2)}) collective-permute-start(bf16[512,1024]{1,0:T(8,128)(2,1)S(1)} %copy-done.6), channel_id=1, source_target_pairs={{0,8},{8,0},{16,24},{24,16},{1,9},{9,1},{17,25},{25,17},{2,10},{10... | collective-permute-start | bytes 3145736 | tf_op jit(solution)/shard_map/ppermute | solution.py:257
  401.4 18.4 %collective-permute-start.15 = (bf16[256,1024]{1,0:T(8,128)(2,1)S(1)}, bf16[256,1024]{1,0:T(8,128)(2,1)S(1)}, u32[]{:S(2)}, u32[]{:S(2)}) collective-permute-start(bf16[256,1024]{1,0:T(8,128)(2,1)S(1)} %copy-done.13), channel_id=1, source_target_pairs={{0,8},{8,0},{16,24},{24,16},{1,9},{9,1},{17,25},{25,17},{2,10},{10... | collective-permute-start | bytes 1572872 | tf_op jit(solution)/shard_map/ppermute | solution.py:257
  409.0 11.3 %collective-permute-start.17 = (bf16[256,1024]{1,0:T(8,128)(2,1)S(1)}, bf16[256,1024]{1,0:T(8,128)(2,1)S(1)}, u32[]{:S(2)}, u32[]{:S(2)}) collective-permute-start(bf16[256,1024]{1,0:T(8,128)(2,1)S(1)} %collective-permute-done.16), channel_id=1, source_target_pairs={{0,8},{8,0},{16,24},{24,16},{1,9},{9,1},{17,25},{25,17},{2,10},{10... | collective-permute-start | bytes 1572872 | tf_op jit(solution)/shard_map/ppermute | solution.py:257
  409.0 12.8 %copy-start.9 = (bf16[4,8,32,1280]{3,2,1,0:T(8,128)(2,1)S(1)}, bf16[4,8,32,1280]{3,2,1,0:T(8,128)(2,1)}, u32[]{:S(2)}) copy-start(bf16[4,8,32,1280]{3,2,1,0:T(8,128)(2,1)} %get-tuple-element.23) | copy-start | bytes 7864324
  409.0 25.3 %slice-start.9 = ((s8[5242880]{0:T(1024)(128)(4,1)}), s8[1048576]{0:T(1024)(128)(4,1)S(1)}, s32[]{:S(2)}) async-start(s8[5242880]{0:T(1024)(128)(4,1)} %bitcast.67), calls=%async_computation.13 | async-start | bytes 2097152
  419.7 26.1 %collective-permute-start.4 = (bf16[512,1024]{1,0:T(8,128)(2,1)S(1)}, bf16[512,1024]{1,0:T(8,128)(2,1)S(1)}, u32[]{:S(2)}, u32[]{:S(2)}) collective-permute-start(bf16[512,1024]{1,0:T(8,128)(2,1)S(1)} %copy-done.4), channel_id=1, source_target_pairs={{0,8},{8,0},{16,24},{24,16},{1,9},{9,1},{17,25},{25,17},{2,10},{10... | collective-permute-start | bytes 3145736 | tf_op jit(solution)/shard_map/ppermute | solution.py:257
  420.3 13.9 %collective-permute-start.6 = (bf16[256,1024]{1,0:T(8,128)(2,1)S(1)}, bf16[256,1024]{1,0:T(8,128)(2,1)S(1)}, u32[]{:S(2)}, u32[]{:S(2)}) collective-permute-start(bf16[256,1024]{1,0:T(8,128)(2,1)S(1)} %get-tuple-element.28), channel_id=1, source_target_pairs={{0,16},{8,24},{16,0},{24,8},{1,17},{9,25},{17,1},{25,9},{2,18},{10... | collective-permute-start | bytes 1572872 | tf_op jit(solution)/shard_map/ppermute | solution.py:250
  421.8 12.5 %copy-start.12 = (bf16[512,1024]{1,0:T(8,128)(2,1)S(1)}, bf16[512,1024]{1,0:T(8,128)(2,1)}, u32[]{:S(2)}) copy-start(bf16[512,1024]{1,0:T(8,128)(2,1)} %get-tuple-element.24) | copy-start | bytes 3145732
  424.8 18.1 %collective-permute-start.5 = (bf16[256,1024]{1,0:T(8,128)(2,1)S(1)}, bf16[256,1024]{1,0:T(8,128)(2,1)S(1)}, u32[]{:S(2)}, u32[]{:S(2)}) collective-permute-start(bf16[256,1024]{1,0:T(8,128)(2,1)S(1)} %get-tuple-element.28), channel_id=1, source_target_pairs={{0,8},{8,0},{16,24},{24,16},{1,9},{9,1},{17,25},{25,17},{2,10},{10... | collective-permute-start | bytes 1572872 | tf_op jit(solution)/shard_map/ppermute | solution.py:257
  434.2 8.7 %collective-permute-start.7 = (bf16[256,1024]{1,0:T(8,128)(2,1)S(1)}, bf16[256,1024]{1,0:T(8,128)(2,1)S(1)}, u32[]{:S(2)}, u32[]{:S(2)}) collective-permute-start(bf16[256,1024]{1,0:T(8,128)(2,1)S(1)} %collective-permute-done.6), channel_id=1, source_target_pairs={{0,8},{8,0},{16,24},{24,16},{1,9},{9,1},{17,25},{25,17},{2,10},{10... | collective-permute-start | bytes 1572872 | tf_op jit(solution)/shard_map/ppermute | solution.py:257
  434.2 11.6 %slice-start.6 = ((s8[5242880]{0:T(1024)(128)(4,1)}), s8[4194304]{0:T(1024)(128)(4,1)S(1)}, s32[]{:S(2)}) async-start(s8[5242880]{0:T(1024)(128)(4,1)} %bitcast.64), calls=%async_computation.10 | async-start | bytes 8388608
  445.8 19.3 %copy-start = (bf16[64,5120]{1,0:T(8,128)(2,1)S(1)}, bf16[64,5120]{1,0:T(8,128)(2,1)}, u32[]{:S(2)}) copy-start(bf16[64,5120]{1,0:T(8,128)(2,1)} %reduce-scatter.3.cloned.1.call-done.refs_2_) | copy-start | bytes 1966084
  (12 other events, 99.0 us)
Sparse Core Ops, SparseCore 0:
  209.3 136.8 reduce-scatter.2
  394.4 70.7 reduce-scatter.4

commit v3 on v1

--- a/solution.py
+++ b/solution.py
@@ -44,9 +44,16 @@
         pl.semaphore_signal(barrier, inc=1, device_id=(partner(t, j, n_tok), h), device_id_type=MESH)
     pl.semaphore_wait(barrier, n_tok + jnp.where(z > 0, 1, 0) + jnp.where(z < lines - 1, 1, 0))
 
-    def ag(a, src, s, way, dev):
+    rows = x_ref.shape[0]
+    late = rows // 6 if rows % 96 == 0 else 0
+    spans = ((0, rows - late), (rows - late, late)) if late else ((0, rows),)
+    both = tuple(range(len(spans)))
+
+    def ag(a, src, s, way, dev, part=0):
+        lo, n = spans[part]
         return pltpu.make_async_remote_copy(
-            src_ref=src, dst_ref=fulls[a].at[s], send_sem=ag_send.at[a, way, s], recv_sem=ag_recv.at[a, s],
+            src_ref=src.at[pl.ds(lo, n)], dst_ref=fulls[a].at[s, pl.ds(lo, n)],
+            send_sem=ag_send.at[a, part, way, s], recv_sem=ag_recv.at[a, part, s],
             device_id=(t, dev), device_id_type=MESH,
         )
 
@@ -78,42 +85,60 @@
 
         @pl.when(z < lines - 1)
         def _():
-            ag(a, src, h, 0, h + 2).start()
+            for part in both:
+                ag(a, src, h, 0, h + 2, part).start()
 
         @pl.when(z > 0)
         def _():
-            ag(a, src, h, 1, h - 2).start()
-
-        ag(a, src, h, 2, other).start()
+            for part in both:
+                ag(a, src, h, 1, h - 2, part).start()
+
+        for part in both[::-1]:
+            ag(a, src, h, 2, other, part).start()
     for a in range(2):
         full_own(a).start()
         send_cols(a, mine[a], h)
 
+    def pass_on(a, s, way, part):
+        src = fulls[a].at[s]
+        if way == 0:
+            @pl.when(z < lines - 1)
+            def _():
+                ag(a, src, s, 0, h + 2, part).start()
+        else:
+            @pl.when(z > 0)
+            def _():
+                ag(a, src, s, 1, h - 2, part).start()
+
+    if late:
+        for a in range(2):
+            ag(a, fulls[a].at[other], other, 2, other, 1).wait_recv()
+            pass_on(a, other, 0, 1)
+            pass_on(a, other, 1, 1)
+
+    def own_line(a, s, way):
+        for part in both:
+            ag(a, fulls[a].at[s], s, way, other, part).wait_recv()
+            pass_on(a, s, way, part)
+        ag(a, fulls[a].at[s], s, 2, other).start()
+        send_cols(a, fulls[a].at[s], s)
+
+    def other_line(a, s, way):
+        if late:
+            ag(a, fulls[a].at[s], s, way, other, 1).wait_recv()
+            pass_on(a, s, way, 1)
+        ag(a, fulls[a].at[s], s, 2, other).wait_recv()
+        send_cols(a, fulls[a].at[s], s)
+
     for d in range(1, lines):
         for a in range(2):
             @pl.when(z - d >= 0)
             def _():
-                s = h - 2 * d
-                ag(a, fulls[a].at[s], s, 0, h + 2).wait_recv()
-
-                @pl.when(z < lines - 1)
-                def _():
-                    ag(a, fulls[a].at[s], s, 0, h + 2).start()
-
-                ag(a, fulls[a].at[s], s, 2, other).start()
-                send_cols(a, fulls[a].at[s], s)
+                own_line(a, h - 2 * d, 0)
 
             @pl.when(z + d < lines)
             def _():
-                s = h + 2 * d
-                ag(a, fulls[a].at[s], s, 1, h - 2).wait_recv()
-
-                @pl.when(z > 0)
-                def _():
-                    ag(a, fulls[a].at[s], s, 1, h - 2).start()
-
-                ag(a, fulls[a].at[s], s, 2, other).start()
-                send_cols(a, fulls[a].at[s], s)
+                own_line(a, h + 2 * d, 1)
 
         for a in range(2):
             if d == 1:
@@ -122,30 +147,35 @@
 
             @pl.when(z - d >= 0)
             def _():
-                s = other - 2 * d
-                ag(a, fulls[a].at[s], s, 2, other).wait_recv()
-                send_cols(a, fulls[a].at[s], s)
+                other_line(a, other - 2 * d, 0)
 
             @pl.when(z + d < lines)
             def _():
-                s = other + 2 * d
-                ag(a, fulls[a].at[s], s, 2, other).wait_recv()
-                send_cols(a, fulls[a].at[s], s)
+                other_line(a, other + 2 * d, 1)
 
     for a in range(2):
         full_own(a).wait()
         for zz in range(lines):
             s = zz * 2 + y
+            crossing = zz * 2 + 1 - y
 
             @pl.when(jnp.logical_and(zz <= z, z < lines - 1))
             def _():
-                ag(a, fulls[a].at[s], s, 0, h + 2).wait_send()
+                for part in both:
+                    ag(a, fulls[a].at[s], s, 0, h + 2, part).wait_send()
+                if late:
+                    ag(a, fulls[a].at[crossing], crossing, 0, h + 2, 1).wait_send()
 
             @pl.when(jnp.logical_and(zz >= z, z > 0))
             def _():
-                ag(a, fulls[a].at[s], s, 1, h - 2).wait_send()
+                for part in both:
+                    ag(a, fulls[a].at[s], s, 1, h - 2, part).wait_send()
+                if late:
+                    ag(a, fulls[a].at[crossing], crossing, 1, h - 2, 1).wait_send()
 
             ag(a, fulls[a].at[s], s, 2, other).wait_send()
+        if late:
+            ag(a, fulls[a].at[h], h, 2, other, 1).wait_send()
         for s in range(n_hid):
             own(a, fulls[a].at[s], s).wait()
             for j in range(1, n_tok):
@@ -166,8 +196,8 @@
         out_specs=(anywhere,) * 4,
         scratch_shapes=[
             pltpu.SemaphoreType.DMA((2, n_hid + 1)),
-            pltpu.SemaphoreType.DMA((2, 3, n_hid)),
-            pltpu.SemaphoreType.DMA((2, n_hid)),
+            pltpu.SemaphoreType.DMA((2, 2, 3, n_hid)),
+            pltpu.SemaphoreType.DMA((2, 2, n_hid)),
             pltpu.SemaphoreType.DMA((2, n_tok, n_hid)),
             pltpu.SemaphoreType.DMA((2, n_tok, n_hid)),
         ],

time: 449 us -> 435 us (0.969)
  Pallas kernels: 210 us -> 197 us
    pallas_call x1, Pallas kernels: 210 us -> 197 us  [gather(): pl.pallas_call(functools.partial(gather_kernel, n_tok, n_hid), out_shape=...]
  transfers between devices with their start and end apart: 10 -> 10, of which waited for: 3 -> 3; matrix products, arithmetic and copies ran while one was open for 11% -> 12% of each run, Pallas kernels for 0% -> 0%
where the time goes in v3:
time: 435 us; the launch traced here: 434 us
  Pallas kernels  197 us (45%)
  matrix products  117 us (27%)
  waiting for transfers between devices  93 us (21%)
  between operations  14.1 us (3%)
  local copies, waits for them, and re-layouts  7.17 us (2%)
  starting transfers between devices  4.66 us (1%)
    pallas_call x1, Pallas kernels, gather(): pl.pallas_call(functools.partial(gather_kernel, n_tok, n_hid), out_shape=...  197 us
    ppermute x3, waiting for transfers between devices, body(): lax.ppermute(arr, 'tok', [(d, (d + 2 * k) % n_tok) for d in range(n_tok)])  92.9 us
    dot_general x3, matrix products, weight_sum(): lax.dot_general(columns[:near], jnp.concatenate(parts[:2]), contract_firs...  21.7 us
    dot_general x3, matrix products, weight_sum(): lax.dot_general(columns[near:], jnp.concatenate(parts[2:]), contract_firs...  21.4 us
    dot_general x1, matrix products, body(): up_pre = jnp.dot(inputs_full, up_weight, preferred_element_type=jnp.float32)  16.1 us
    dot_general x1, matrix products, body(): lax.dot_general(grad_up, up_weight, contract_last, preferred_element_type...  15.9 us
    dot_general x1, matrix products, body(): lax.dot_general(grad_gate, gate_weight, contract_last, preferred_element_...  15 us
    dot_general x1, matrix products, body(): lax.dot_general(grads_full, down_weight, contract_last, preferred_element...  14.9 us
  transfers between devices with their start and end apart: 10, of which 3 were waited for; matrix products, arithmetic and copies ran while one was open for 12% of the time, Pallas kernels for 0%

profile of v3, /device:TPU:0, one launch (start us, length us, event | category | flops | bytes accessed | tf_op | source)
XLA Modules:
  0.0 434.4 jit_solution(5508297345401695797)
XLA Ops:
  7.2 0.0 reduce-scatter.2.cloned.1.call-start
  7.2 0.7 iota_compare_fusion
  8.0 0.9 and_reduce_fusion
  8.9 196.6 %gather_rows_and_columns.1 = (bf16[8,96,5120]{2,1,0:T(8,128)(2,1)}, bf16[8,96,5120]{2,1,0:T(8,128)(2,1)}, bf16[4,8,96,1280]{3,2,1,0:T(8,128)(2,1)}, bf16[4,8,96,1280]{3,2,1,0:T(8,128)(2,1)}) custom-call(bf16[96,5120]{1,0:T(8,128)(2,1)} %x_ref.1, bf16[96,5120]{1,0:T(8,128)(2,1)} %g_ref.1), custom_call_target="tpu_custom_call" | custom-call | tf_op jit(solution)/shard_map/gather_rows_and_columns/pallas_call | solution.py:192
  205.5 12.2 %fusion.32 = f32[768,1024]{1,0:T(8,128)S(1)} fusion(bf16[768,5120]{1,0:T(8,128)(2,1)} %bitcast.39, bf16[5120,1024]{1,0:T(8,128)(2,1)} %param.9), kind=kOutput, calls=%fused_computation.44 | convolution fusion | flops 8053063680 | bytes 21495808 | tf_op jit(solution)/shard_map/dot_general | solution.py:245
  217.7 0.3 broadcast_in_dim.2
  217.9 14.9 %bitcast_multiply_fusion.1 = f32[768,1024]{1,0:T(8,128)} fusion(f32[96,8,8,128]{3,2,1,0:T(8,128)S(1)} %bitcast.37, bf16[768,5120]{1,0:T(8,128)(2,1)} %bitcast.41, bf16[1024,5120]{1,0:T(8,128)(2,1)} %param.11), kind=kOutput, calls=%fused_computation.5 | convolution fusion | flops 8053850112 | bytes 24641536 | tf_op jit(solution)/shard_map/dot_general | solution.py:247
  232.9 16.1 %fusion.1 = (bf16[768,1024]{1,0:T(8,128)(2,1)S(1)}, bf16[768,1024]{1,0:T(8,128)(2,1)S(1)}, bf16[768,1024]{1,0:T(8,128)(2,1)}) fusion(f32[96,8,8,128]{3,2,1,0:T(8,128)S(1)} %bitcast.38, f32[768,1024]{1,0:T(8,128)S(1)} %fusion.32, f32[768,1024]{1,0:T(8,128)} %bitcast_multiply_fusion.1, bf16[768,5120]{1,0:T(8,128)(2,1)} %bitcast.40, bf16[5120,1024]{1,0:T(8,128)(2,1)} %param.10), kind=kOutput, calls=%fused_computation.7 | convolution fusion | flops 8065646592 | bytes 32505856 | tf_op jit(solution)/shard_map/dot_general | solution.py:246
  249.0 15.0 %fusion.33 = f32[768,5120]{1,0:T(8,128)} fusion(bf16[768,1024]{1,0:T(8,128)(2,1)S(1)} %get-tuple-element.17, bf16[5120,1024]{1,0:T(8,128)(2,1)} %param.9), kind=kOutput, calls=%fused_computation.45 | convolution fusion | flops 8053063680 | bytes 27787264 | tf_op jit(solution)/shard_map/dot_general | solution.py:252
  264.1 15.9 %add_convert_fusion = bf16[768,5120]{1,0:T(8,128)(2,1)} fusion(f32[768,5120]{1,0:T(8,128)} %fusion.33, bf16[768,1024]{1,0:T(8,128)(2,1)} %get-tuple-element.18, bf16[5120,1024]{1,0:T(8,128)(2,1)} %param.10), kind=kOutput, calls=%fused_computation | convolution fusion | flops 8060928000 | bytes 35651584 | tf_op jit(solution)/shard_map/dot_general | solution.py:258
  279.9 0.0 reduce-scatter.2.cloned.1.call-update
  279.9 0.1 collective-permute-start.7
  280.0 2.0 collective-permute-start.3
  282.0 0.4 collective-permute-start.4
  282.4 1.7 collective-permute-start.1
  284.1 0.0 collective-permute-start
  284.1 6.9 %fusion.30 = (bf16[2,8,96,1280]{3,2,1,0:T(8,128)(2,1)S(1)}, bf16[2,8,96,1280]{3,2,1,0:T(8,128)(2,1)S(1)}, bf16[2,8,96,1280]{3,2,1,0:T(8,128)(2,1)S(1)}, bf16[2,8,96,1280]{3,2,1,0:T(8,128)(2,1)S(1)}) fusion(bf16[4,8,96,1280]{3,2,1,0:T(8,128)(2,1)} %get-tuple-element.11, bf16[4,8,96,1280]{3,2,1,0:T(8,128)(2,1)} %get-tuple-element.10), kind=kLoop, calls=%fused_computation.42 | loop fusion | bytes 31457280 | tf_op jit(solution)/shard_map/slice | solution.py:279
  290.9 26.2 %collective-permute-done.7 = bf16[768,1024]{1,0:T(8,128)(2,1)S(1)} collective-permute-done((bf16[768,1024]{1,0:T(8,128)(2,1)S(1)}, bf16[768,1024]{1,0:T(8,128)(2,1)S(1)}, u32[]{:S(2)}, u32[]{:S(2)}) %collective-permute-start.7) | collective-permute-done | bytes 1572896 | tf_op jit(solution)/shard_map/ppermute | solution.py:269
  317.2 0.0 collective-permute-done.3
  317.2 0.5 collective-permute-start.8
  317.7 33.3 %collective-permute-done.4 = bf16[768,1024]{1,0:T(8,128)(2,1)} collective-permute-done((bf16[768,1024]{1,0:T(8,128)(2,1)}, bf16[768,1024]{1,0:T(8,128)(2,1)}, u32[]{:S(2)}, u32[]{:S(2)}) %collective-permute-start.4) | collective-permute-done | bytes 1572896 | tf_op jit(solution)/shard_map/ppermute | solution.py:269
  351.0 0.0 collective-permute-start.5
  351.0 33.4 %collective-permute-done.1 = bf16[768,1024]{1,0:T(8,128)(2,1)} collective-permute-done((bf16[768,1024]{1,0:T(8,128)(2,1)S(1)}, bf16[768,1024]{1,0:T(8,128)(2,1)}, u32[]{:S(2)}, u32[]{:S(2)}) %collective-permute-start.1) | collective-permute-done | bytes 1572896 | tf_op jit(solution)/shard_map/ppermute | solution.py:269
  384.4 0.0 collective-permute-start.2
  384.4 8.0 %fusion.9 = f32[1280,1024]{1,0:T(8,128)} fusion(bf16[1536,1280]{1,0:T(8,128)(2,1)S(1)} %bitcast.35, bf16[768,1024]{1,0:T(8,128)(2,1)} %collective-permute-done.3, bf16[768,1024]{1,0:T(8,128)(2,1)} %get-tuple-element.18), kind=kOutput, calls=%fused_computation.15 | convolution fusion | flops 4032823296 | bytes 12320768 | tf_op jit(solution)/shard_map/dot_general | solution.py:275
  392.4 0.0 collective-permute-done
  392.4 7.5 %fusion.2 = f32[1280,1024]{1,0:T(8,128)} fusion(bf16[1536,1280]{1,0:T(8,128)(2,1)S(1)} %bitcast.36, bf16[768,1024]{1,0:T(8,128)(2,1)} %collective-permute-done, bf16[768,1024]{1,0:T(8,128)(2,1)S(1)} %get-tuple-element.17), kind=kOutput, calls=%fused_computation.8 | convolution fusion | flops 4032823296 | bytes 12320768 | tf_op jit(solution)/shard_map/dot_general | solution.py:275
  399.9 6.2 %fusion.16 = f32[1024,1280]{1,0:T(8,128)} fusion(bf16[1536,1280]{1,0:T(8,128)(2,1)S(1)} %bitcast.34, bf16[768,1024]{1,0:T(8,128)(2,1)S(1)} %collective-permute-done.6, bf16[768,1024]{1,0:T(8,128)(2,1)S(1)} %get-tuple-element.16), kind=kOutput, calls=%fused_computation.22 | convolution fusion | flops 4032823296 | bytes 12320768 | tf_op jit(solution)/shard_map/dot_general | solution.py:275
  406.1 0.0 collective-permute-done.5
  406.1 8.0 %multiply_convert_fusion.1 = bf16[1280,1024]{1,0:T(8,128)(2,1)} fusion(f32[1280,1024]{1,0:T(8,128)} %fusion.9, bf16[1536,1280]{1,0:T(8,128)(2,1)S(1)} %bitcast.32, bf16[768,1024]{1,0:T(8,128)(2,1)S(1)} %collective-permute-done.5, bf16[768,1024]{1,0:T(8,128)(2,1)} %collective-permute-done.4), kind=kOutput, calls=%fused_computation.2 | convolution fusion | flops 4036755456 | bytes 14942208 | tf_op jit(solution)/shard_map/dot_general | solution.py:278
  414.2 7.3 %multiply_convert_fusion.2 = bf16[1280,1024]{1,0:T(8,128)(2,1)} fusion(f32[1280,1024]{1,0:T(8,128)S(1)} %bitcast.45, bf16[1536,1280]{1,0:T(8,128)(2,1)S(1)} %bitcast.33, bf16[768,1024]{1,0:T(8,128)(2,1)S(1)} %collective-permute-done.2, bf16[768,1024]{1,0:T(8,128)(2,1)} %collective-permute-done.1), kind=kOutput, calls=%fused_computation.3 | convolution fusion | flops 4036755456 | bytes 14942208 | tf_op jit(solution)/shard_map/dot_general | solution.py:278
  421.5 6.1 %multiply_convert_fusion = bf16[1024,1280]{1,0:T(8,128)(2,1)} fusion(f32[1024,1280]{1,0:T(8,128)S(1)} %bitcast.43, bf16[1536,1280]{1,0:T(8,128)(2,1)S(1)} %bitcast.31, bf16[768,1024]{1,0:T(8,128)(2,1)S(1)} %collective-permute-done.8, bf16[768,1024]{1,0:T(8,128)(2,1)S(1)} %collective-permute-done.7), kind=kOutput, calls=%fused_computation.1 | convolution fusion | flops 4036755456 | bytes 14942208 | tf_op jit(solution)/shard_map/dot_general | solution.py:278
  (17 shorter events, 0.0 us)
Async XLA Ops:
  7.2 420.4 %reduce-scatter.2.cloned.1.call-start = ((), (), s32[]{:S(2)}) async-start(), calls=%async_computation.1 | async-start | bytes 8847360 | tf_op jit(solution)/shard_map/reduce_scatter | solution.py:255
  279.9 37.2 %collective-permute-start.7 = (bf16[768,1024]{1,0:T(8,128)(2,1)S(1)}, bf16[768,1024]{1,0:T(8,128)(2,1)S(1)}, u32[]{:S(2)}, u32[]{:S(2)}) collective-permute-start(bf16[768,1024]{1,0:T(8,128)(2,1)S(1)} %get-tuple-element.16), channel_id=1, source_target_pairs={{0,16},{8,24},{16,0},{24,8},{1,17},{9,25},{17,1},{25,9},{2,18},{10... | collective-permute-start | bytes 4718600 | tf_op jit(solution)/shard_map/ppermute | solution.py:269
  280.0 37.2 %collective-permute-start.3 = (bf16[768,1024]{1,0:T(8,128)(2,1)}, bf16[768,1024]{1,0:T(8,128)(2,1)}, u32[]{:S(2)}, u32[]{:S(2)}) collective-permute-start(bf16[768,1024]{1,0:T(8,128)(2,1)} %get-tuple-element.18), channel_id=1, source_target_pairs={{0,8},{8,0},{16,24},{24,16},{1,9},{9,1},{17,25},{25,17},{2,10},{10... | collective-permute-start | bytes 4718600 | tf_op jit(solution)/shard_map/ppermute | solution.py:270
  282.0 69.0 %collective-permute-start.4 = (bf16[768,1024]{1,0:T(8,128)(2,1)}, bf16[768,1024]{1,0:T(8,128)(2,1)}, u32[]{:S(2)}, u32[]{:S(2)}) collective-permute-start(bf16[768,1024]{1,0:T(8,128)(2,1)} %get-tuple-element.18), channel_id=1, source_target_pairs={{0,16},{8,24},{16,0},{24,8},{1,17},{9,25},{17,1},{25,9},{2,18},{10... | collective-permute-start | bytes 4718600 | tf_op jit(solution)/shard_map/ppermute | solution.py:269
  282.4 102.0 %collective-permute-start.1 = (bf16[768,1024]{1,0:T(8,128)(2,1)S(1)}, bf16[768,1024]{1,0:T(8,128)(2,1)}, u32[]{:S(2)}, u32[]{:S(2)}) collective-permute-start(bf16[768,1024]{1,0:T(8,128)(2,1)S(1)} %get-tuple-element.17), channel_id=1, source_target_pairs={{0,16},{8,24},{16,0},{24,8},{1,17},{9,25},{17,1},{25,9},{2,18},{10... | collective-permute-start | bytes 4718600 | tf_op jit(solution)/shard_map/ppermute | solution.py:269
  284.1 108.4 %collective-permute-start = (bf16[768,1024]{1,0:T(8,128)(2,1)S(1)}, bf16[768,1024]{1,0:T(8,128)(2,1)}, u32[]{:S(2)}, u32[]{:S(2)}) collective-permute-start(bf16[768,1024]{1,0:T(8,128)(2,1)S(1)} %get-tuple-element.17), channel_id=1, source_target_pairs={{0,8},{8,0},{16,24},{24,16},{1,9},{9,1},{17,25},{25,17},{2,10},{10... | collective-permute-start | bytes 4718600 | tf_op jit(solution)/shard_map/ppermute | solution.py:270
  317.2 82.7 %collective-permute-start.6 = (bf16[768,1024]{1,0:T(8,128)(2,1)S(1)}, bf16[768,1024]{1,0:T(8,128)(2,1)S(1)}, u32[]{:S(2)}, u32[]{:S(2)}) collective-permute-start(bf16[768,1024]{1,0:T(8,128)(2,1)S(1)} %get-tuple-element.16), channel_id=1, source_target_pairs={{0,8},{8,0},{16,24},{24,16},{1,9},{9,1},{17,25},{25,17},{2,10},{10... | collective-permute-start | bytes 4718600 | tf_op jit(solution)/shard_map/ppermute | solution.py:270
  317.2 104.3 %collective-permute-start.8 = (bf16[768,1024]{1,0:T(8,128)(2,1)S(1)}, bf16[768,1024]{1,0:T(8,128)(2,1)S(1)}, u32[]{:S(2)}, u32[]{:S(2)}) collective-permute-start(bf16[768,1024]{1,0:T(8,128)(2,1)S(1)} %collective-permute-done.7), channel_id=1, source_target_pairs={{0,8},{8,0},{16,24},{24,16},{1,9},{9,1},{17,25},{25,17},{2,10},{10... | collective-permute-start | bytes 4718600 | tf_op jit(solution)/shard_map/ppermute | solution.py:270
  351.0 55.1 %collective-permute-start.5 = (bf16[768,1024]{1,0:T(8,128)(2,1)}, bf16[768,1024]{1,0:T(8,128)(2,1)S(1)}, u32[]{:S(2)}, u32[]{:S(2)}) collective-permute-start(bf16[768,1024]{1,0:T(8,128)(2,1)} %collective-permute-done.4), channel_id=1, source_target_pairs={{0,8},{8,0},{16,24},{24,16},{1,9},{9,1},{17,25},{25,17},{2,10},{10... | collective-permute-start | bytes 4718600 | tf_op jit(solution)/shard_map/ppermute | solution.py:270
  384.4 29.8 %collective-permute-start.2 = (bf16[768,1024]{1,0:T(8,128)(2,1)}, bf16[768,1024]{1,0:T(8,128)(2,1)S(1)}, u32[]{:S(2)}, u32[]{:S(2)}) collective-permute-start(bf16[768,1024]{1,0:T(8,128)(2,1)} %collective-permute-done.1), channel_id=1, source_target_pairs={{0,8},{8,0},{16,24},{24,16},{1,9},{9,1},{17,25},{25,17},{2,10},{10... | collective-permute-start | bytes 4718600 | tf_op jit(solution)/shard_map/ppermute | solution.py:270
  399.9 14.3 %slice-start.2 = ((s8[5242880]{0:T(1024)(128)(4,1)}), s8[1048576]{0:T(1024)(128)(4,1)S(1)}, s32[]{:S(2)}) async-start(s8[5242880]{0:T(1024)(128)(4,1)} %bitcast.44), calls=%async_computation.4 | async-start | bytes 2097152
  406.1 8.1 %slice-start.3 = ((s8[5242880]{0:T(1024)(128)(4,1)}), s8[4194304]{0:T(1024)(128)(4,1)S(1)}, s32[]{:S(2)}) async-start(s8[5242880]{0:T(1024)(128)(4,1)} %bitcast.44), calls=%async_computation.5 | async-start | bytes 8388608
  406.1 15.4 %slice-start = ((s8[5242880]{0:T(1024)(128)(4,1)}), s8[1048576]{0:T(1024)(128)(4,1)S(1)}, s32[]{:S(2)}) async-start(s8[5242880]{0:T(1024)(128)(4,1)} %bitcast.42), calls=%async_computation.2 | async-start | bytes 2097152
  414.2 7.3 %slice-start.1 = ((s8[5242880]{0:T(1024)(128)(4,1)}), s8[4194304]{0:T(1024)(128)(4,1)S(1)}, s32[]{:S(2)}) async-start(s8[5242880]{0:T(1024)(128)(4,1)} %bitcast.42), calls=%async_computation.3 | async-start | bytes 8388608
Sparse Core Ops, SparseCore 0:
  280.1 139.6 reduce-scatter.1
